TPU v7x, 32 devices: a whole 2x2x4 slice. The times are simulated.
32 devices in a mesh: slab: 8 (over y, x, core), pencil: 4 (over z).
Axes of the slice: x: 2, y: 2, z: 4, core: 2. Of those that a mesh axis runs over, the one named last changes fastest.
Arguments:
- surface_eta: float32 [2048, 4096], P('pencil', 'slab'), may hold values from -1.2 to 1.2
- surface_potential: float32 [2048, 4096], P('pencil', 'slab'), may hold values from -1.8 to 1.8
- velocity: float32 [3, 128, 64, 128], P(None, 'slab', 'pencil'), may hold values from -3 to 3
- send_point: int32 [8, 4, 8, 256], P('slab', 'pencil'), may hold values from 0 to 262143
- send_count: int32 [8, 4, 8], P('slab', 'pencil'), may hold values from 1 to 256, as said below
- stencil: int32 [4, 128, 64], P(None, 'slab', 'pencil'), may hold values from 0 to 2047, as said below
- interp_weight: float32 [4, 128, 64], P(None, 'slab', 'pencil'), may hold values from 0.2 to 1
Outputs:
- surface_vertical: float32 [2048, 4096], P('pencil', 'slab')
- velocity_next: float32 [3, 128, 64, 128], P(None, 'slab', 'pencil')
Inputs may be any that keep to these rules, and one draw needn't show every extreme that they name: `send_count`: equals 256 toward the first and the last 1 slabs d, at most 64 toward the others. stencil[q, x, y] = r * 256 + j with j < send_count[r, y // 16, x // 16].
All inputs are finite; a program needn't handle non-finite values.
Results may differ from a plain program's by a relative error of at most 0.00015.
Values sent between devices are 32-bit elements; how exact they have to be, the bound alone decides.
A program may use at most 256 MiB of HBM per device.

v0:
```python
import math

import jax
import jax.numpy as jnp
from jax import lax
from jax.sharding import PartitionSpec as P

NXW = 4096
NYW = 2048
STEPS = 2


TIME_STEP = 0.2
VISCOSITY = 0.6
DEPTH_RATE = 3.0


def padded_2(shard, sides, width):
    for axis, dim in sides:
        size, length = (lax.axis_size(axis), shard.shape[dim])
        up = [(i, (i + 1) % size) for i in range(size - 1)]
        down = [(j, i) for i, j in up]
        last = lax.slice_in_dim(shard, length - width, length, axis=dim)
        leading = lax.slice_in_dim(shard, 0, width, axis=dim)
        before = lax.ppermute(last, axis, up)
        after = lax.ppermute(leading, axis, down)
        shard = jnp.concatenate([before, shard, after], axis=dim)
    return shard


def hartley_last(values):
    length = values.shape[-1]
    outer_len = 1 << (length.bit_length() - 1) // 2
    inner_len = length // outer_len
    blocks = values.reshape(values.shape[:-1] + (outer_len, inner_len))
    outer_idx = jnp.arange(outer_len, dtype=jnp.int32)
    inner_idx = jnp.arange(inner_len, dtype=jnp.int32)
    angle_a = (
        2.0
        * math.pi
        / outer_len
        * (outer_idx[:, None] * outer_idx[None, :] % outer_len).astype(jnp.float32)
    )
    angle_t = (
        2.0
        * math.pi
        / length
        * (outer_idx[:, None] * inner_idx[None, :] % length).astype(jnp.float32)
    )
    angle_b = (
        2.0
        * math.pi
        / inner_len
        * (inner_idx[:, None] * inner_idx[None, :] % inner_len).astype(jnp.float32)
    )
    highest = lax.Precision.HIGHEST
    real_a = jnp.einsum("...ab,ak->...kb", blocks, jnp.cos(angle_a), precision=highest)
    imag_a = -jnp.einsum("...ab,ak->...kb", blocks, jnp.sin(angle_a), precision=highest)
    cos_t = jnp.cos(angle_t)
    sin_t = jnp.sin(angle_t)
    real_t = real_a * cos_t + imag_a * sin_t
    imag_t = imag_a * cos_t - real_a * sin_t
    cos_b = jnp.cos(angle_b)
    sin_b = jnp.sin(angle_b)
    real_b = jnp.einsum("...kb,bm->...km", real_t, cos_b, precision=highest) + jnp.einsum(
        "...kb,bm->...km", imag_t, sin_b, precision=highest
    )
    imag_b = jnp.einsum("...kb,bm->...km", imag_t, cos_b, precision=highest) - jnp.einsum(
        "...kb,bm->...km", real_t, sin_b, precision=highest
    )
    return jnp.swapaxes(real_b - imag_b, -1, -2).reshape(values.shape)


def hartley_rows(values):
    return jnp.moveaxis(hartley_last(jnp.moveaxis(values, -2, -1)), -1, -2)


def to_columns(values):
    return lax.all_to_all(values, "slab", split_axis=1, concat_axis=2, tiled=True)


def from_columns(values):
    return lax.all_to_all(values, "slab", split_axis=2, concat_axis=1, tiled=True)


def to_rows(values):
    return lax.all_to_all(values, "pencil", split_axis=2, concat_axis=1, tiled=True)


def from_rows(values):
    return lax.all_to_all(values, "pencil", split_axis=1, concat_axis=2, tiled=True)


def tile_pass(values):
    return from_rows(hartley_rows(to_rows(from_columns(hartley_last(to_columns(values))))))


def wavenumber(index, length):
    folded = jnp.minimum(index, length - index)
    return 2.0 * math.pi / length * folded.astype(jnp.float32)


def ramp_weight(distance, reach_len):
    ratio = jnp.clip(1.0 - distance / reach_len, 0.0, 1.0)
    return ratio * ratio


def blend_weight(pos_x, pos_y, total_x, total_y, reach_x, reach_y):
    along_x = jnp.maximum(ramp_weight(pos_x, reach_x), ramp_weight(total_x - 1.0 - pos_x, reach_x))
    across = jnp.maximum(ramp_weight(pos_y, reach_y), ramp_weight(total_y - 1.0 - pos_y, reach_y))
    return jnp.maximum(along_x[:, None], across[None, :])[:, :, None]


def advance(velocity, padded, relax_weight, target):
    shifted = jnp.pad(padded, ((0, 0), (0, 0), (0, 0), (1, 1)))
    components = []
    for component in range(3):
        current = shifted[component]
        plus_x = current[2:, 1:-1, 1:-1]
        minus_x = current[:-2, 1:-1, 1:-1]
        plus_y = current[1:-1, 2:, 1:-1]
        minus_y = current[1:-1, :-2, 1:-1]
        plus_z = current[1:-1, 1:-1, 2:]
        minus_z = current[1:-1, 1:-1, :-2]
        laplace = (
            plus_x + minus_x + (plus_y + minus_y) + (plus_z + minus_z) - 6.0 * velocity[component]
        )
        advect = (
            velocity[0] * (plus_x - minus_x)
            + velocity[1] * (plus_y - minus_y)
            + velocity[2] * (plus_z - minus_z)
        )
        predicted = velocity[component] + TIME_STEP * (VISCOSITY * laplace - 0.5 * advect)
        components.append((1.0 - relax_weight) * predicted + relax_weight * target[component])
    return jnp.stack(components)


def on_device(
    surface_eta, surface_potential, velocity, send_point, send_count, stencil, interp_weight
):
    slab_count = lax.axis_size("slab")
    pencil_count = lax.axis_size("pencil")
    slab_index = lax.axis_index("slab")
    pencil_index = lax.axis_index("pencil")
    tile_rows, tile_cols = surface_eta.shape
    norm_scale = 1.0 / (NXW * NYW)
    wave_y = wavenumber(pencil_index * tile_rows + jnp.arange(tile_rows, dtype=jnp.int32), NYW)[
        :, None
    ]
    wave_x = wavenumber(slab_index * tile_cols + jnp.arange(tile_cols, dtype=jnp.int32), NXW)[
        None, :
    ]
    magnitude = jnp.sqrt(wave_x * wave_x + wave_y * wave_y)
    first_mult = magnitude * norm_scale
    second_mult = magnitude * magnitude * norm_scale
    third_mult = magnitude * magnitude * magnitude * norm_scale
    spectrum = tile_pass(surface_potential[None])[0]
    first_set = tile_pass(
        jnp.stack([spectrum * first_mult, spectrum * second_mult, spectrum * third_mult])
    )
    slope_one = first_set[0]
    curve_one = first_set[1]
    cubic_one = first_set[2]
    potential_two = -surface_eta * slope_one
    spectrum = tile_pass(potential_two[None])[0]
    second_set = tile_pass(jnp.stack([spectrum * first_mult, spectrum * second_mult]))
    slope_two = second_set[0]
    curve_two = second_set[1]
    potential_three = -surface_eta * slope_two - 0.5 * surface_eta * surface_eta * curve_one
    spectrum = tile_pass(potential_three[None])[0]
    slope_three = tile_pass((spectrum * first_mult)[None])[0]
    vertical = (
        slope_one
        + slope_two
        + surface_eta * curve_one
        + slope_three
        + surface_eta * curve_two
        + 0.5 * surface_eta * surface_eta * cubic_one
    )
    point_lists = send_point[0, 0]
    counts = send_count[0, 0]
    capacity = point_lists.shape[1]
    values = jnp.stack([surface_eta, vertical]).reshape(2, tile_rows * tile_cols)
    picked = values[:, point_lists]
    live_mask = jnp.arange(capacity, dtype=jnp.int32)[None, :] < counts[:, None]
    picked = jnp.where(live_mask[None], picked, 0.0)
    arrived = lax.all_to_all(picked, "slab", split_axis=1, concat_axis=1, tiled=True).reshape(
        2, slab_count * capacity
    )
    sampled = arrived[:, stencil]
    shares = interp_weight / jnp.sum(interp_weight, axis=0)
    surface_at = jnp.sum(sampled * shares[None], axis=1)
    block_x = velocity.shape[1]
    block_y = velocity.shape[2]
    depth_cells = velocity.shape[3]
    zone_slabs = max(1, slab_count // 16)
    pos_x = (slab_index * block_x + jnp.arange(block_x, dtype=jnp.int32)).astype(jnp.float32)
    pos_y = (pencil_index * block_y + jnp.arange(block_y, dtype=jnp.int32)).astype(jnp.float32)
    relax_weight = blend_weight(
        pos_x,
        pos_y,
        float(block_x * slab_count),
        float(block_y * pencil_count),
        float(zone_slabs * block_x),
        float(block_y),
    )
    levels = jnp.arange(depth_cells, dtype=jnp.float32)
    depth_decay = jnp.exp(-DEPTH_RATE * (depth_cells - 1.0 - levels) / depth_cells)
    target = jnp.stack(
        [
            surface_at[0][:, :, None] * depth_decay,
            jnp.zeros((block_x, block_y, depth_cells), jnp.float32),
            surface_at[1][:, :, None] * depth_decay,
        ]
    )
    for substep in range(STEPS):
        padded = padded_2(velocity, (("slab", 1), ("pencil", 2)), 1)
        velocity = advance(velocity, padded, relax_weight, target)
    return (vertical, velocity)


def solution(mesh):
    in_specs = (
        P("pencil", "slab"),
        P("pencil", "slab"),
        P(None, "slab", "pencil", None),
        P("slab", "pencil", None, None),
        P("slab", "pencil", None),
        P(None, "slab", "pencil"),
        P(None, "slab", "pencil"),
    )
    out_specs = (P("pencil", "slab"), P(None, "slab", "pencil", None))
    return jax.shard_map(
        on_device, mesh=mesh, in_specs=in_specs, out_specs=out_specs, check_vma=False
    )
```

profile of v0, /device:TPU:0, one launch (start us, length us, event | category | flops | bytes accessed | tf_op | source)
XLA Modules:
  0.0 1516.5 jit_solution(4196024412822149209)
XLA Ops:
  3.5 5.2 all-to-all-start
  9.2 15.0 all-to-all-done
  35.7 13.9 subtract_bitcast_fusion.9
  53.5 19.4 %reduce.6 = f32[4096,64]{1,0:T(8,128)} reduce(f32[4096,1,64]{2,1,0:T(1,128)S(1)} %bitcast.921, f32[]{:T(128)} %broadcast.1238), dimensions={1}, to_apply=%bitcast.850.reduce_sub_computation | reduce | bytes 2097156
  75.4 17.8 %all_to_all.401 = f32[8,1,32768]{2,1,0:T(1,128)S(1)} all-to-all(f32[8,1,32768]{2,1,0:T(1,128)S(1)} %reshape.911), channel_id=1, replica_groups=mesh['slab'=8,'pencil'=4] {'slab'}, dimensions={0} | all-to-all | bytes 2097152 | tf_op jit(solution)/shard_map/all_to_all | solution.py:83
  102.4 5.1 all-to-all-start.2
  107.6 24.9 %all-to-all-done.2 = f32[1,512,512]{1,0,2:T(1,128)S(1)} async-done(((f32[1,512,512]{1,0,2:T(1,128)}), f32[1,512,512]{1,0,2:T(1,128)S(1)}, u32[]{:S(2)}, u32[]{:S(2)}) %all-to-all-start.2) | async-done | bytes 1048608 | tf_op jit(solution)/shard_map/all_to_all | solution.py:87
  149.2 25.2 %all-to-all-done.3 = f32[1,2048,128]{2,0,1:T(1,128)S(1)} async-done(((f32[1,2048,128]{2,0,1:T(1,128)}), f32[1,2048,128]{2,0,1:T(1,128)S(1)}, u32[]{:S(2)}, u32[]{:S(2)}) %all-to-all-start.3) | async-done | bytes 1048608 | tf_op jit(solution)/shard_map/all_to_all | solution.py:91
  179.1 52.7 %all_to_all.402 = f32[3,512,512]{2,0,1:T(4,128)S(1)} all-to-all(f32[3,512,512]{2,0,1:T(4,128)} %copy.557), channel_id=1, replica_groups=mesh['slab'=8,'pencil'=4] {'slab'}, dimensions={1} | all-to-all | bytes 6291456 | tf_op jit(solution)/shard_map/all_to_all | solution.py:79
  238.1 8.3 fusion.210
  246.4 6.2 fusion.222
  252.6 7.6 fusion.2
  260.3 7.8 fusion.4
  268.1 7.6 fusion
  275.7 12.0 subtract_bitcast_fusion
  287.7 10.9 copy.723
  298.6 10.2 reshape.913
  308.8 41.4 %all_to_all.403 = f32[8,1,98304]{2,1,0:T(1,128)S(1)} all-to-all(f32[8,1,98304]{2,1,0:T(1,128)} %reshape.913), channel_id=1, replica_groups=mesh['slab'=8,'pencil'=4] {'slab'}, dimensions={0} | all-to-all | bytes 6291456 | tf_op jit(solution)/shard_map/all_to_all | solution.py:83
  350.2 11.1 reduce.8
  361.3 9.9 reshape.914
  371.2 6.5 copy.725
  381.2 96.5 %all_to_all.404 = f32[3,512,512]{1,0,2:T(4,128)S(1)} all-to-all(f32[3,512,512]{1,0,2:T(4,128)} %copy.570), channel_id=1, replica_groups=mesh['slab'=8,'pencil'=4] {'pencil'}, dimensions={2} | all-to-all | bytes 6291456 | tf_op jit(solution)/shard_map/all_to_all | solution.py:87
  487.1 5.2 add_bitcast_fusion
  492.3 5.3 fusion.16
  497.6 4.9 fusion.18
  502.5 5.1 fusion.20
  507.6 5.5 subtract_bitcast_fusion.2
  514.9 10.0 copy.580
  525.0 5.0 all-to-all-start.7
  530.3 91.9 %all-to-all-done.7 = f32[3,2048,128]{2,0,1:T(4,128)} async-done(((f32[3,2048,128]{2,0,1:T(4,128)}), f32[3,2048,128]{2,0,1:T(4,128)}, u32[]{:S(2)}, u32[]{:S(2)}) %all-to-all-start.7) | async-done | bytes 3145760 | tf_op jit(solution)/shard_map/all_to_all | solution.py:91
  628.7 18.8 %all_to_all.405 = f32[1,512,512]{2,0,1:T(1,128)S(1)} all-to-all(f32[1,512,512]{2,0,1:T(1,128)} %copy.584), channel_id=1, replica_groups=mesh['slab'=8,'pencil'=4] {'slab'}, dimensions={1} | all-to-all | bytes 2097152 | tf_op jit(solution)/shard_map/all_to_all | solution.py:79
  668.9 19.4 %reduce.9 = f32[4096,64]{1,0:T(8,128)} reduce(f32[4096,1,64]{2,1,0:T(1,128)S(1)} %bitcast.923, f32[]{:T(128)} %broadcast.1238), dimensions={1}, to_apply=%bitcast.854.reduce_sub_computation | reduce | bytes 2097156
  690.8 17.8 %all_to_all.406 = f32[8,1,32768]{2,1,0:T(1,128)S(1)} all-to-all(f32[8,1,32768]{2,1,0:T(1,128)S(1)} %reshape.915), channel_id=1, replica_groups=mesh['slab'=8,'pencil'=4] {'slab'}, dimensions={0} | all-to-all | bytes 2097152 | tf_op jit(solution)/shard_map/all_to_all | solution.py:83
  708.6 4.5 reduce.10
  721.4 28.2 %all_to_all.407 = f32[1,512,512]{1,0,2:T(1,128)S(1)} all-to-all(f32[1,512,512]{1,0,2:T(1,128)S(1)} %copy.594), channel_id=1, replica_groups=mesh['slab'=8,'pencil'=4] {'pencil'}, dimensions={2} | all-to-all | bytes 2097152 | tf_op jit(solution)/shard_map/all_to_all | solution.py:87
  761.3 27.9 %all_to_all.408 = f32[1,2048,128]{2,0,1:T(1,128)S(1)} all-to-all(f32[1,2048,128]{2,0,1:T(1,128)S(1)} %bitcast.954), channel_id=1, replica_groups=mesh['slab'=8,'pencil'=4] {'pencil'}, dimensions={1} | all-to-all | bytes 2097152 | tf_op jit(solution)/shard_map/all_to_all | solution.py:91
  792.7 30.1 %all_to_all.409 = f32[2,512,512]{2,0,1:T(2,128)S(1)} all-to-all(f32[2,512,512]{2,0,1:T(2,128)} %copy.605), channel_id=1, replica_groups=mesh['slab'=8,'pencil'=4] {'slab'}, dimensions={1} | all-to-all | bytes 4194304 | tf_op jit(solution)/shard_map/all_to_all | solution.py:79
  826.8 5.9 fusion.206
  849.0 5.9 subtract_bitcast_fusion.1
  854.9 7.6 copy.736
  862.5 7.1 reshape.917
  869.6 30.2 %all_to_all.410 = f32[8,1,65536]{2,1,0:T(1,128)} all-to-all(f32[8,1,65536]{2,1,0:T(1,128)S(1)} %reshape.917), channel_id=1, replica_groups=mesh['slab'=8,'pencil'=4] {'slab'}, dimensions={0} | all-to-all | bytes 4194304 | tf_op jit(solution)/shard_map/all_to_all | solution.py:83
  899.8 7.2 reduce.11
  907.0 5.0 reshape.918
  912.0 5.2 copy.738
  919.7 51.4 %all_to_all.411 = f32[2,512,512]{1,0,2:T(2,128)S(1)} all-to-all(f32[2,512,512]{1,0,2:T(2,128)} %copy.618), channel_id=1, replica_groups=mesh['slab'=8,'pencil'=4] {'pencil'}, dimensions={2} | all-to-all | bytes 4194304 | tf_op jit(solution)/shard_map/all_to_all | solution.py:87
  997.0 8.5 copy.628
  1005.6 4.6 all-to-all-start.15
  1010.5 47.0 %all-to-all-done.15 = f32[2,2048,128]{2,0,1:T(2,128)} async-done(((f32[2,2048,128]{2,0,1:T(2,128)}), f32[2,2048,128]{2,0,1:T(2,128)}, u32[]{:S(2)}, u32[]{:S(2)}) %all-to-all-start.15) | async-done | bytes 2097184 | tf_op jit(solution)/shard_map/all_to_all | solution.py:91
  1066.0 18.3 %all_to_all.412 = f32[1,512,512]{2,0,1:T(1,128)S(1)} all-to-all(f32[1,512,512]{2,0,1:T(1,128)S(1)} %copy.635), channel_id=1, replica_groups=mesh['slab'=8,'pencil'=4] {'slab'}, dimensions={1} | all-to-all | bytes 2097152 | tf_op jit(solution)/shard_map/all_to_all | solution.py:79
  1105.6 19.4 %reduce.12 = f32[4096,64]{1,0:T(8,128)} reduce(f32[4096,1,64]{2,1,0:T(1,128)S(1)} %bitcast.927, f32[]{:T(128)} %broadcast.1238), dimensions={1}, to_apply=%bitcast.858.reduce_sub_computation | reduce | bytes 2097156
  1127.5 17.8 %all_to_all.413 = f32[8,1,32768]{2,1,0:T(1,128)S(1)} all-to-all(f32[8,1,32768]{2,1,0:T(1,128)S(1)} %reshape.919), channel_id=1, replica_groups=mesh['slab'=8,'pencil'=4] {'slab'}, dimensions={0} | all-to-all | bytes 2097152 | tf_op jit(solution)/shard_map/all_to_all | solution.py:83
  1145.3 4.5 reduce.13
  1158.0 28.0 %all_to_all.414 = f32[1,512,512]{1,0,2:T(1,128)S(1)} all-to-all(f32[1,512,512]{1,0,2:T(1,128)S(1)} %copy.645), channel_id=1, replica_groups=mesh['slab'=8,'pencil'=4] {'pencil'}, dimensions={2} | all-to-all | bytes 2097152 | tf_op jit(solution)/shard_map/all_to_all | solution.py:87
  1197.7 27.7 %all_to_all.415 = f32[1,2048,128]{2,0,1:T(1,128)S(1)} all-to-all(f32[1,2048,128]{2,0,1:T(1,128)S(1)} %bitcast.959), channel_id=1, replica_groups=mesh['slab'=8,'pencil'=4] {'pencil'}, dimensions={1} | all-to-all | bytes 2097152 | tf_op jit(solution)/shard_map/all_to_all | solution.py:91
  1227.0 17.8 %all_to_all.416 = f32[1,512,512]{2,0,1:T(1,128)S(1)} all-to-all(f32[1,512,512]{2,0,1:T(1,128)S(1)} %copy.656), channel_id=1, replica_groups=mesh['slab'=8,'pencil'=4] {'slab'}, dimensions={1} | all-to-all | bytes 2097152 | tf_op jit(solution)/shard_map/all_to_all | solution.py:79
  1266.0 19.4 %reduce.14 = f32[4096,64]{1,0:T(8,128)} reduce(f32[4096,1,64]{2,1,0:T(1,128)S(1)} %bitcast.928, f32[]{:T(128)} %broadcast.1238), dimensions={1}, to_apply=%bitcast.860.reduce_sub_computation | reduce | bytes 2097156
  1287.9 17.8 %all_to_all.417 = f32[8,1,32768]{2,1,0:T(1,128)S(1)} all-to-all(f32[8,1,32768]{2,1,0:T(1,128)S(1)} %reshape.921), channel_id=1, replica_groups=mesh['slab'=8,'pencil'=4] {'slab'}, dimensions={0} | all-to-all | bytes 2097152 | tf_op jit(solution)/shard_map/all_to_all | solution.py:83
  1305.7 4.5 reduce.15
  1327.2 21.3 %all-to-all-done.22 = f32[1,512,512]{1,0,2:T(1,128)S(1)} async-done(((f32[1,512,512]{1,0,2:T(1,128)}), f32[1,512,512]{1,0,2:T(1,128)S(1)}, u32[]{:S(2)}, u32[]{:S(2)}) %all-to-all-start.22) | async-done | bytes 1048608 | tf_op jit(solution)/shard_map/all_to_all | solution.py:87
  1373.3 9.4 collective-permute-done.2
  1402.3 58.1 %copy.681 = f32[2,262144]{0,1:T(8,128)} copy(f32[2,262144]{1,0:T(2,128)S(1)} %pad_maximum_fusion.2) | data formatting | bytes 4194304 | tf_op jit(solution)/shard_map/stack | solution.py:183
  1460.4 20.6 %gather_fusion = f32[2048,2]{1,0:T(8,128)S(1)} fusion(f32[2,262144]{0,1:T(8,128)} %copy.681, s32[2048]{0:T(1024)S(1)} %broadcast_clamp_fusion), kind=kCustom, calls=%fused_computation | custom fusion | bytes 40960 | tf_op jit(solution)/shard_map/gather | solution.py:184
  1499.5 8.4 collective-permute-start.6
  (259 shorter events, 341.0 us)
Async XLA Ops:
  3.5 20.6 %all-to-all-start = ((f32[1,512,512]{2,0,1:T(1,128)}), f32[1,512,512]{2,0,1:T(1,128)S(1)}, u32[]{:S(2)}, u32[]{:S(2)}) async-start(f32[1,512,512]{2,0,1:T(1,128)} %broadcast_in_dim.16), calls=%async_computation | async-start | bytes 2097152 | tf_op jit(solution)/shard_map/all_to_all | solution.py:79
  102.4 30.1 %all-to-all-start.2 = ((f32[1,512,512]{1,0,2:T(1,128)}), f32[1,512,512]{1,0,2:T(1,128)S(1)}, u32[]{:S(2)}, u32[]{:S(2)}) async-start(f32[1,512,512]{1,0,2:T(1,128)} %copy.546), calls=%async_computation.2 | async-start | bytes 2097152 | tf_op jit(solution)/shard_map/all_to_all | solution.py:87
  145.2 29.1 %all-to-all-start.3 = ((f32[1,2048,128]{2,0,1:T(1,128)}), f32[1,2048,128]{2,0,1:T(1,128)S(1)}, u32[]{:S(2)}, u32[]{:S(2)}) async-start(f32[1,2048,128]{2,0,1:T(1,128)} %bitcast.46), calls=%async_computation.3 | async-start | bytes 2097152 | tf_op jit(solution)/shard_map/all_to_all | solution.py:91
  238.1 8.3 copy-start
  525.0 5.0 copy-start.9
  525.0 97.3 %all-to-all-start.7 = ((f32[3,2048,128]{2,0,1:T(4,128)}), f32[3,2048,128]{2,0,1:T(4,128)}, u32[]{:S(2)}, u32[]{:S(2)}) async-start(f32[3,2048,128]{2,0,1:T(4,128)} %copy.580), calls=%async_computation.7 | async-start | bytes 8388608 | tf_op jit(solution)/shard_map/all_to_all | solution.py:91
  626.5 2.2 copy-start.2
  826.8 5.9 copy-start.1
  1005.6 4.6 copy-start.13
  1005.6 51.9 %all-to-all-start.15 = ((f32[2,2048,128]{2,0,1:T(2,128)}), f32[2,2048,128]{2,0,1:T(2,128)}, u32[]{:S(2)}, u32[]{:S(2)}) async-start(f32[2,2048,128]{2,0,1:T(2,128)} %copy.628), calls=%async_computation.15 | async-start | bytes 4194304 | tf_op jit(solution)/shard_map/all_to_all | solution.py:91
  1010.5 51.7 %copy-start.4 = (f32[1,512,4,128]{1,3,2,0:T(8,128)}, f32[1,512,4,128]{1,3,2,0:T(8,128)S(1)}, u32[]{:S(2)}) copy-start(f32[1,512,4,128]{1,3,2,0:T(8,128)S(1)} %copy.631) | copy-start | bytes 3145732
  1062.3 1.4 copy-start.6
  1317.7 9.3 copy-start.20
  1317.7 9.3 copy-start.19
  1319.6 28.8 %all-to-all-start.22 = ((f32[1,512,512]{1,0,2:T(1,128)}), f32[1,512,512]{1,0,2:T(1,128)S(1)}, u32[]{:S(2)}, u32[]{:S(2)}) async-start(f32[1,512,512]{1,0,2:T(1,128)} %copy.666), calls=%async_computation.22 | async-start | bytes 2097152 | tf_op jit(solution)/shard_map/all_to_all | solution.py:87
  1323.9 41.8 %collective-permute-start = (f32[3,1,16,128]{3,2,1,0:T(8,128)S(1)}, f32[3,1,16,128]{3,2,1,0:T(8,128)S(1)}, u32[]{:S(2)}, u32[]{:S(2)}) collective-permute-start(f32[3,1,16,128]{3,2,1,0:T(8,128)S(1)} %get-tuple-element.47), channel_id=1, source_target_pairs={{0,4},{4,8},{8,12},{12,16},{16,20},{20,24},{24,28},{1,5},{5,9},{9,... | collective-permute-start | bytes 73736 | tf_op jit(solution)/shard_map/ppermute | solution.py:25
  1325.2 40.5 %collective-permute-start.1 = (f32[3,1,16,128]{3,2,1,0:T(8,128)S(1)}, f32[3,1,16,128]{3,2,1,0:T(8,128)S(1)}, u32[]{:S(2)}, u32[]{:S(2)}) collective-permute-start(f32[3,1,16,128]{3,2,1,0:T(8,128)S(1)} %get-tuple-element.46), channel_id=1, source_target_pairs={{4,0},{8,4},{12,8},{16,12},{20,16},{24,20},{28,24},{5,1},{9,5},{13... | collective-permute-start | bytes 73736 | tf_op jit(solution)/shard_map/ppermute | solution.py:26
  1359.5 6.0 copy-start.18
  1359.6 6.0 copy-start.21
  1359.6 6.1 copy-start.7
  1361.2 10.0 copy-start.10
  1361.2 29.9 %all-to-all-start.23 = ((f32[1,2048,128]{2,0,1:T(1,128)}), f32[1,2048,128]{2,0,1:T(1,128)}, u32[]{:S(2)}, u32[]{:S(2)}) async-start(f32[1,2048,128]{2,0,1:T(1,128)} %bitcast.946), calls=%async_computation.23 | async-start | bytes 2097152 | tf_op jit(solution)/shard_map/all_to_all | solution.py:91
  1365.8 16.8 %collective-permute-start.2 = (f32[3,18,1,128]{3,2,1,0:T(1,128)S(1)}, f32[3,18,1,128]{3,2,1,0:T(1,128)S(1)}, u32[]{:S(2)}, u32[]{:S(2)}) collective-permute-start(f32[3,18,1,128]{3,2,1,0:T(1,128)S(1)} %get-tuple-element.42), channel_id=1, source_target_pairs={{0,1},{1,2},{2,3},{4,5},{5,6},{6,7},{8,9},{9,10},{10,11},{12,13},{... | collective-permute-start | bytes 82952 | tf_op jit(solution)/shard_map/ppermute | solution.py:25
  1369.7 13.0 collective-permute-start.3
  1373.3 11.2 copy-start.12
  1385.8 7.9 copy-start.3
  1385.8 7.9 copy-start.5
  1397.6 2.8 copy-start.14
  1399.2 1.1 copy-start.11
  1402.3 83.0 %copy-start.8 = (f32[3,16,16,128]{3,2,1,0:T(8,128)S(1)}, f32[3,16,16,128]{3,2,1,0:T(8,128)}, u32[]{:S(2)}) copy-start(f32[3,16,16,128]{3,2,1,0:T(8,128)} %param.9) | copy-start | bytes 1179652
  1402.3 83.0 %copy-start.17 = (f32[18,18,130]{2,1,0:T(8,128)S(1)}, f32[18,18,130]{2,1,0:T(8,128)}, u32[]{:S(2)}) copy-start(f32[18,18,130]{2,1,0:T(8,128)} %get-tuple-element.33) | copy-start | bytes 505444
  1481.3 12.3 copy-start.16
  1482.0 8.0 all-to-all-start.24
  1485.6 8.3 copy-start.15
  1494.3 3.0 collective-permute-start.4
  1496.0 3.5 collective-permute-start.5
  1499.5 10.0 collective-permute-start.6
  1508.0 5.8 collective-permute-start.7
where the time goes:
time: 1530 us; the launch traced here: 1520 us
  blocking collectives  540 us (35%)
  local copies, waits for them, and re-layouts  303 us (20%)
  waiting for transfers between devices  248 us (16%)
  matrix products  239 us (16%)
  other arithmetic  128 us (8%)
  starting transfers between devices  56 us (4%)
    all_to_all x4, blocking collectives, to_rows(): lax.all_to_all(values, 'pencil', split_axis=2, concat_axis=1, tiled=True)  204 us
    all_to_all x4, waiting for transfers between devices, from_rows(): lax.all_to_all(values, 'pencil', split_axis=1, concat_axis=2, tiled=True)  167 us
    all_to_all x6, blocking collectives, from_columns(): lax.all_to_all(values, 'slab', split_axis=2, concat_axis=1, tiled=True)  143 us
    all_to_all x5, blocking collectives, to_columns(): lax.all_to_all(values, 'slab', split_axis=1, concat_axis=2, tiled=True)  138 us
    unnamed x5, other arithmetic  77.4 us
    unnamed x71, local copies, waits for them, and re-layouts  62.8 us
    another operation x1, local copies, waits for them, and re-layouts, on_device(): jnp.stack([surface_eta, vertical]).reshape(2, tile_rows * tile_cols)  58.1 us
    all_to_all x2, blocking collectives, from_rows(): lax.all_to_all(values, 'pencil', split_axis=1, concat_axis=2, tiled=True)  55.7 us
  transfers between devices with their start and end apart: 16, of which 12 were waited for; matrix products, arithmetic and copies ran while one was open for 2% of the time, Pallas kernels for 0%

commit v1 on v0

v1 whole, which is shorter than its diff:
```python
import math

import jax
import jax.numpy as jnp
import numpy as np
from jax import lax
from jax.sharding import PartitionSpec as P

NXW = 4096
NYW = 2048
STEPS = 2
INNER = 256


TIME_STEP = 0.2
VISCOSITY = 0.6
DEPTH_RATE = 3.0

HIGH = lax.Precision.HIGH
BOTH = ("pencil", "slab")


def real_dft(parts):
    size = len(parts)
    if size == 2:
        return [(parts[0] + parts[1], None), (parts[0] - parts[1], None)]
    even = real_dft(parts[0::2])
    odd = real_dft(parts[1::2])
    half = size // 2
    result = [None] * (half + 1)
    for k in range(size // 4 + 1):
        (even_re, even_im), (odd_re, odd_im) = even[k], odd[k]
        if k == 0:
            result[0] = (even_re + odd_re, None)
            result[half] = (even_re - odd_re, None)
        elif 4 * k == size:
            result[k] = (even_re, -odd_re)
        else:
            c, s = math.cos(2.0 * math.pi * k / size), math.sin(2.0 * math.pi * k / size)
            turned_re = c * odd_re + s * odd_im
            turned_im = c * odd_im - s * odd_re
            result[k] = (even_re + turned_re, even_im + turned_im)
            result[half - k] = (even_re - turned_re, turned_im - even_im)
    return result


def outer_dft(parts):
    bins = real_dft(list(parts))
    out = [bins[0][0], bins[-1][0]]
    for re, im in bins[1:-1]:
        out += [re, im]
    return tuple(out)


def outer_dft_transposed(pieces):
    shapes = tuple(jax.ShapeDtypeStruct(piece.shape, piece.dtype) for piece in pieces)
    return jax.linear_transpose(lambda *parts: outer_dft(parts), *shapes)(tuple(pieces))


def tables(length):
    outer = length // INNER
    within = np.arange(INNER)
    blocks = np.zeros((outer // 2, 2 * INNER, 2 * INNER), np.float64)
    order = np.zeros((outer // 2, 2 * INNER), np.int32)
    for b in range(outer // 2):
        for side in range(2):
            if b == 0:
                first = 0 if side == 0 else outer // 2
            else:
                first = b if side == 0 else outer - b
            freq = first + outer * within
            angle = 2.0 * math.pi / length * ((within[:, None] * freq[None, :]) % length)
            cos, sin = np.cos(angle), np.sin(angle)
            columns = slice(side * INNER, (side + 1) * INNER)
            order[b, columns] = freq
            if b == 0:
                blocks[b, columns, columns] = cos + sin
            else:
                sign = 1.0 if side == 0 else -1.0
                blocks[b, :INNER, columns] = cos + sin
                blocks[b, INNER:, columns] = sign * (sin - cos)
    return blocks.astype(np.float32), np.minimum(order, length - order)


def rows_forward(values, blocks, device_count):
    rows, length = values.shape
    pieces = outer_dft([values[:, i : i + INNER] for i in range(0, length, INNER)])
    stacked = jnp.stack(
        [jnp.concatenate(pieces[2 * b : 2 * b + 2], axis=1) for b in range(len(pieces) // 2)]
    )
    spectrum = jnp.einsum("brk,bkn->brn", stacked, blocks, precision=HIGH)
    columns = length // device_count
    spectrum = spectrum.reshape(spectrum.shape[0], rows, 2 * INNER // columns, columns)
    return spectrum.transpose(0, 2, 1, 3).reshape(device_count, rows, columns)


def rows_inverse(values, blocks):
    device_count, rows, columns = values.shape
    grouped = values.reshape(blocks.shape[0], 2 * INNER // columns, rows, columns)
    grouped = grouped.transpose(0, 2, 1, 3).reshape(blocks.shape[0], rows, 2 * INNER)
    stacked = jnp.einsum("brn,bkn->brk", grouped, blocks, precision=HIGH)
    pieces = []
    for b in range(blocks.shape[0]):
        pieces += [stacked[b, :, :INNER], stacked[b, :, INNER:]]
    return jnp.concatenate(outer_dft_transposed(pieces), axis=1)


def columns_forward(values, blocks):
    pieces = outer_dft([values[i : i + INNER] for i in range(0, values.shape[0], INNER)])
    stacked = jnp.concatenate(pieces, axis=0).reshape(
        blocks.shape[0], 2 * INNER, values.shape[1]
    )
    return jnp.einsum("bkn,bkc->bnc", blocks, stacked, precision=HIGH)


def columns_inverse(values, blocks):
    stacked = jnp.einsum("bkn,bnc->bkc", blocks, values, precision=HIGH)
    pieces = []
    for b in range(blocks.shape[0]):
        pieces += [stacked[b, :INNER], stacked[b, INNER:]]
    return jnp.concatenate(outer_dft_transposed(pieces), axis=0)


def exchange(values):
    return lax.all_to_all(values, BOTH, split_axis=0, concat_axis=0, tiled=True)


def ramp_weight(distance, reach_len):
    ratio = jnp.clip(1.0 - distance / reach_len, 0.0, 1.0)
    return ratio * ratio


def blend_weight(pos_x, pos_y, total_x, total_y, reach_x, reach_y):
    along_x = jnp.maximum(ramp_weight(pos_x, reach_x), ramp_weight(total_x - 1.0 - pos_x, reach_x))
    across = jnp.maximum(ramp_weight(pos_y, reach_y), ramp_weight(total_y - 1.0 - pos_y, reach_y))
    return jnp.maximum(along_x[:, None], across[None, :])[:, :, None]


def neighbours(shard, axis, dim):
    size, length = lax.axis_size(axis), shard.shape[dim]
    up = [(i, i + 1) for i in range(size - 1)]
    down = [(i + 1, i) for i in range(size - 1)]
    before = lax.ppermute(lax.slice_in_dim(shard, length - 1, length, axis=dim), axis, up)
    after = lax.ppermute(lax.slice_in_dim(shard, 0, 1, axis=dim), axis, down)
    minus = jnp.concatenate([before, lax.slice_in_dim(shard, 0, length - 1, axis=dim)], axis=dim)
    plus = jnp.concatenate([lax.slice_in_dim(shard, 1, length, axis=dim), after], axis=dim)
    return minus, plus


def predict(velocity):
    minus_x, plus_x = neighbours(velocity, "slab", 1)
    minus_y, plus_y = neighbours(velocity, "pencil", 2)
    padded = jnp.pad(velocity, ((0, 0), (0, 0), (0, 0), (1, 1)))
    minus_z, plus_z = padded[..., :-2], padded[..., 2:]
    laplace = plus_x + minus_x + (plus_y + minus_y) + (plus_z + minus_z) - 6.0 * velocity
    advect = (
        velocity[0] * (plus_x - minus_x)
        + velocity[1] * (plus_y - minus_y)
        + velocity[2] * (plus_z - minus_z)
    )
    return velocity + TIME_STEP * (VISCOSITY * laplace - 0.5 * advect)


def on_device(
    surface_eta, surface_potential, velocity, send_point, send_count, stencil, interp_weight
):
    slab_count = lax.axis_size("slab")
    pencil_count = lax.axis_size("pencil")
    device_count = slab_count * pencil_count
    slab_index = lax.axis_index("slab")
    pencil_index = lax.axis_index("pencil")
    tile_rows, tile_cols = surface_eta.shape
    rows = NYW // device_count
    columns = NXW // device_count
    row_table, row_order = tables(NXW)
    column_table, column_order = tables(NYW)
    row_blocks, column_blocks = jnp.asarray(row_table), jnp.asarray(column_table)

    both = jnp.stack([surface_potential, surface_eta]).reshape(2, slab_count, rows, tile_cols)
    both = lax.all_to_all(both, "slab", split_axis=1, concat_axis=1, tiled=True)
    both = both.transpose(0, 2, 1, 3).reshape(2, rows, NXW)
    potential, eta = both[0], both[1]

    own = pencil_index * slab_count + slab_index
    wave_x = 2.0 * math.pi / NXW * jnp.asarray(row_order.reshape(-1)).astype(jnp.float32)
    wave_x = lax.dynamic_slice(wave_x, (own * columns,), (columns,))
    wave_y = 2.0 * math.pi / NYW * jnp.asarray(column_order).astype(jnp.float32)[:, :, None]
    magnitude = jnp.sqrt(wave_x * wave_x + wave_y * wave_y)
    first_mult = magnitude * (1.0 / (NXW * NYW))
    second_mult = magnitude * first_mult
    third_mult = magnitude * second_mult

    def forward(field):
        arrived = exchange(rows_forward(field, row_blocks, device_count))
        return columns_forward(arrived.reshape(NYW, columns), column_blocks)

    def inverse(spectrum):
        field = columns_inverse(spectrum, column_blocks)
        return rows_inverse(exchange(field.reshape(device_count, rows, columns)), row_blocks)

    spectrum = forward(potential)
    slope_one = inverse(spectrum * first_mult)
    curve_one = inverse(spectrum * second_mult)
    cubic_one = inverse(spectrum * third_mult)
    spectrum = forward(-eta * slope_one)
    slope_two = inverse(spectrum * first_mult)
    curve_two = inverse(spectrum * second_mult)
    spectrum = forward(-eta * slope_two - 0.5 * eta * eta * curve_one)
    slope_three = inverse(spectrum * first_mult)
    vertical = (
        slope_one
        + slope_two
        + eta * curve_one
        + slope_three
        + eta * curve_two
        + 0.5 * eta * eta * cubic_one
    )
    vertical = vertical.reshape(rows, slab_count, tile_cols).transpose(1, 0, 2)
    vertical = lax.all_to_all(vertical, "slab", split_axis=0, concat_axis=0, tiled=True)
    vertical = vertical.reshape(tile_rows, tile_cols)

    points = send_point[0, 0]
    capacity = points.shape[1]
    counts = send_count[0, 0]
    flat_points = points.reshape(-1)
    live = (jnp.arange(capacity, dtype=jnp.int32)[None, :] < counts[:, None]).reshape(-1)
    row_pick = (
        (flat_points // tile_cols)[:, None] == jnp.arange(tile_rows, dtype=jnp.int32)[None, :]
    ).astype(jnp.float32)
    column_pick = (flat_points % tile_cols)[:, None] == jnp.arange(tile_cols, dtype=jnp.int32)[
        None, :
    ]
    column_pick = column_pick & live[:, None]

    def pick(tile):
        picked_rows = jnp.dot(row_pick, tile, precision=HIGH)
        return jnp.sum(jnp.where(column_pick, picked_rows, 0.0), axis=1)

    picked = jnp.stack([pick(surface_eta), pick(vertical)]).reshape(2, slab_count, capacity)
    arrived = lax.all_to_all(picked, "slab", split_axis=1, concat_axis=1, tiled=True).reshape(
        2, slab_count * capacity
    )
    block_x, block_y, depth_cells = velocity.shape[1:]
    shares = interp_weight / jnp.sum(interp_weight, axis=0)
    slots = jnp.arange(slab_count * capacity, dtype=jnp.int32)[:, None]
    mixing = 0.0
    for q in range(stencil.shape[0]):
        mixing = mixing + jnp.where(
            slots == stencil[q].reshape(1, -1), shares[q].reshape(1, -1), 0.0
        )
    surface_at = jnp.dot(arrived, mixing, precision=lax.Precision.HIGHEST)
    surface_at = surface_at.reshape(2, block_x, block_y)

    zone_slabs = max(1, slab_count // 16)
    pos_x = (slab_index * block_x + jnp.arange(block_x, dtype=jnp.int32)).astype(jnp.float32)
    pos_y = (pencil_index * block_y + jnp.arange(block_y, dtype=jnp.int32)).astype(jnp.float32)
    relax_weight = blend_weight(
        pos_x,
        pos_y,
        float(block_x * slab_count),
        float(block_y * pencil_count),
        float(zone_slabs * block_x),
        float(block_y),
    )
    levels = jnp.arange(depth_cells, dtype=jnp.float32)
    depth_decay = jnp.exp(-DEPTH_RATE * (depth_cells - 1.0 - levels) / depth_cells)
    target = jnp.stack(
        [
            surface_at[0][:, :, None] * depth_decay,
            jnp.zeros((block_x, block_y, depth_cells), jnp.float32),
            surface_at[1][:, :, None] * depth_decay,
        ]
    )
    for substep in range(STEPS):
        velocity = (1.0 - relax_weight) * predict(velocity) + relax_weight * target
    return (vertical, velocity)


def solution(mesh):
    in_specs = (
        P("pencil", "slab"),
        P("pencil", "slab"),
        P(None, "slab", "pencil", None),
        P("slab", "pencil", None, None),
        P("slab", "pencil", None),
        P(None, "slab", "pencil"),
        P(None, "slab", "pencil"),
    )
    out_specs = (P("pencil", "slab"), P(None, "slab", "pencil", None))
    return jax.shard_map(
        on_device, mesh=mesh, in_specs=in_specs, out_specs=out_specs, check_vma=False
    )
```

time: 1530 us -> 432 us (0.28)
  blocking collectives: 540 us -> 31.6 us
  local copies, waits for them, and re-layouts: 303 us -> 45.5 us
  matrix products: 239 us -> 98.3 us
  waiting for transfers between devices: 248 us -> 108 us
  other arithmetic: 128 us -> 71.7 us
    all_to_all x17 -> x1, blocking collectives: 540 us -> 31.6 us  [on_device(): both = lax.all_to_all(both, 'slab', split_axis=1, concat_axis=1, tiled=True)]
    dot_general x72 -> x21, matrix products: 239 us -> 98.3 us  [the longest x6 44.6 us: rows_inverse(): stacked = jnp.einsum('brn,bkn->brk', grouped, blocks, precision=HIGH)]
    all_to_all x7 -> x10, waiting for transfers between devices: 228 us -> 103 us  [the longest x9 92.7 us: exchange(): return lax.all_to_all(values, BOTH, split_axis=0, concat_axis=0, tiled=True)]
    another operation x7 -> x4, local copies, waits for them, and re-layouts: 70.2 us -> 0.43 us  [the longest x1 58.1 us: on_device(): jnp.stack([surface_eta, vertical]).reshape(2, tile_rows * tile_cols)]
    all_to_all x39 -> x0, local copies, waits for them, and re-layouts: 63.3 us -> none  [the longest x16 35.4 us: from_columns(): lax.all_to_all(values, 'slab', split_axis=2, concat_axis=1, tiled=True)]
    unnamed x71 -> x217, local copies, waits for them, and re-layouts: 62.8 us -> 16.9 us
    all_to_all x6 -> x0, other arithmetic: 35 us -> none  [from_columns(): lax.all_to_all(values, 'slab', split_axis=2, concat_axis=1, tiled=True)]
    unnamed x5 -> x155, other arithmetic: 77.4 us -> 47.5 us
  transfers between devices with their start and end apart: 16 -> 19, of which waited for: 12 -> 11; matrix products, arithmetic and copies ran while one was open for 2% -> 44% of each run, Pallas kernels for 0% -> 0%
where the time goes in v1:
time: 432 us; the launch traced here: 426 us
  waiting for transfers between devices  108 us (25%)
  matrix products  98.3 us (23%)
  other arithmetic  71.7 us (17%)
  starting transfers between devices  67.3 us (16%)
  local copies, waits for them, and re-layouts  45.5 us (11%)
  blocking collectives  31.6 us (7%)
    all_to_all x9, waiting for transfers between devices, exchange(): return lax.all_to_all(values, BOTH, split_axis=0, concat_axis=0, tiled=True)  92.7 us
    unnamed x155, other arithmetic  47.5 us
    dot_general x6, matrix products, rows_inverse(): stacked = jnp.einsum('brn,bkn->brk', grouped, blocks, precision=HIGH)  44.6 us
    all_to_all x9, starting transfers between devices, exchange(): return lax.all_to_all(values, BOTH, split_axis=0, concat_axis=0, tiled=True)  38.1 us
    all_to_all x1, blocking collectives, on_device(): both = lax.all_to_all(both, 'slab', split_axis=1, concat_axis=1, tiled=True)  31.6 us
    dot_general x6, matrix products, columns_inverse(): stacked = jnp.einsum('bkn,bnc->bkc', blocks, values, precision=HIGH)  25.1 us
    unnamed x217, local copies, waits for them, and re-layouts  16.9 us
    ppermute x4, starting transfers between devices, neighbours(): lax.ppermute(lax.slice_in_dim(shard, length - 1, length, axis=dim), axis,...  16.6 us
  transfers between devices with their start and end apart: 19, of which 11 were waited for; matrix products, arithmetic and copies ran while one was open for 44% of the time, Pallas kernels for 0%

profile of v1, /device:TPU:0, one launch (start us, length us, event | category | flops | bytes accessed | tf_op | source)
XLA Modules:
  0.0 426.0 jit_solution(17132571842488829916)
XLA Ops:
  0.6 1.8 pad_maximum_fusion
  2.4 31.6 %all_to_all.60 = f32[2,8,64,512]{3,2,0,1:T(8,128)S(1)} all-to-all(f32[2,8,64,512]{3,2,0,1:T(8,128)S(1)} %pad_maximum_fusion), channel_id=1, replica_groups=mesh['slab'=8,'pencil'=4] {'slab'}, dimensions={1} | all-to-all | bytes 4194304 | tf_op jit(solution)/shard_map/all_to_all | solution.py:180
  38.2 3.2 fusion.244
  42.6 4.0 all-to-all-start.1
  48.5 3.6 collective-permute-start.1
  54.1 5.4 %collective-permute-start.3 = (f32[3,16,1,128]{3,2,1,0:T(1,128)}, f32[3,16,1,128]{3,2,1,0:T(1,128)}, u32[]{:S(2)}, u32[]{:S(2)}) collective-permute-start(f32[3,16,1,128]{3,2,1,0:T(1,128)} %get-tuple-element.359), channel_id=1, source_target_pairs={{0,1},{1,2},{2,3},{4,5},{5,6},{6,7},{8,9},{9,10},{10,11},{12,13},{... | collective-permute-start | bytes 73736 | tf_op jit(solution)/shard_map/ppermute | solution.py:143
  64.3 8.8 %all-to-all-done.1 = f32[32,64,128]{2,1,0:T(8,128)S(1)} async-done(((f32[32,64,128]{2,1,0:T(8,128)}), f32[32,64,128]{2,1,0:T(8,128)S(1)}, u32[]{:S(2)}, u32[]{:S(2)}) %all-to-all-start.1) | async-done | bytes 1048608 | tf_op jit(solution)/shard_map/all_to_all | solution.py:125
  73.6 1.8 copy-done
  75.3 1.8 fusion.245
  77.2 3.8 fusion.16
  80.9 3.8 fusion.23
  84.7 4.3 %fusion.21 = f32[4,512,128]{2,1,0:T(8,128)S(1)} fusion(f32[4,512,512]{1,2,0:T(8,128)S(1)} %copy-done, f32[4,512,128]{2,1,0:T(8,128)S(1)} %fusion.245, f32[4,512]{1,0:T(4,128)S(1)} %copy-done.66, f32[128]{0:T(128)S(1)} %copy-done.85), kind=kOutput, calls=%fused_computation.34 | convolution fusion | flops 806617088 | bytes 6300160 | tf_op jit(solution)/shard_map/bkn,bnc->bkc/dot_general | solution.py:117
  91.7 3.5 all-to-all-start.2
  101.5 19.9 %all-to-all-done.2 = f32[32,64,128]{2,1,0:T(8,128)} async-done(((f32[32,64,128]{2,1,0:T(8,128)}), f32[32,64,128]{2,1,0:T(8,128)}, u32[]{:S(2)}, u32[]{:S(2)}) %all-to-all-start.2) | async-done | bytes 1048608 | tf_op jit(solution)/shard_map/all_to_all | solution.py:125
  121.5 3.7 all-to-all-start.5
  125.2 1.9 copy.79
  127.5 7.3 %fusion.246 = f32[8,64,512]{2,1,0:T(8,128)S(1)} fusion(f32[8,64,512]{2,1,0:T(8,128)S(1)} %reshape.401, f32[8,512,512]{2,1,0:T(8,128)} %constant.100.clone), kind=kOutput, calls=%fused_computation.978 | convolution fusion | flops 805306368 | bytes 10485760 | tf_op jit(solution)/shard_map/brn,bkn->brk/dot_general | solution.py:101
  137.3 14.2 %all-to-all-done.5 = f32[32,64,128]{2,1,0:T(8,128)} async-done(((f32[32,64,128]{2,1,0:T(8,128)}), f32[32,64,128]{2,1,0:T(8,128)}, u32[]{:S(2)}, u32[]{:S(2)}) %all-to-all-start.5) | async-done | bytes 1048608 | tf_op jit(solution)/shard_map/all_to_all | solution.py:125
  151.4 3.9 all-to-all-start.9
  155.4 2.9 copy.77
  158.3 2.6 reshape.409
  161.0 7.7 %fusion.250 = f32[8,64,512]{2,1,0:T(8,128)S(1)} fusion(f32[8,64,512]{2,1,0:T(8,128)} %reshape.409, f32[8,512,512]{2,1,0:T(8,128)} %constant.100.clone), kind=kOutput, calls=%fused_computation.982 | convolution fusion | flops 805306368 | bytes 10485760 | tf_op jit(solution)/shard_map/brn,bkn->brk/dot_general | solution.py:101
  170.6 6.2 %fusion.247 = f32[8,64,512]{2,1,0:T(8,128)S(1)} fusion(f32[8,64,512]{2,1,0:T(8,128)S(1)} %constant_dynamic-update-slice_fusion.40, f32[8,512,512]{2,1,0:T(8,128)} %constant.100.clone), kind=kOutput, calls=%fused_computation.979 | convolution fusion | flops 805306368 | bytes 10485760 | tf_op jit(solution)/shard_map/brk,bkn->brn/dot_general | solution.py:91
  186.2 6.2 %all-to-all-start.3 = ((f32[32,64,128]{2,1,0:T(8,128)}), f32[32,64,128]{2,1,0:T(8,128)S(1)}, u32[]{:S(2)}, u32[]{:S(2)}) async-start(f32[32,64,128]{2,1,0:T(8,128)} %bitcast.2041), calls=%async_computation.3 | async-start | bytes 2097152 | tf_op jit(solution)/shard_map/all_to_all | solution.py:125
  192.4 2.9 copy.74
  195.2 2.6 reshape.420
  197.9 7.7 %fusion.255 = f32[8,64,512]{2,1,0:T(8,128)S(1)} fusion(f32[8,64,512]{2,1,0:T(8,128)} %reshape.420, f32[8,512,512]{2,1,0:T(8,128)} %constant.100.clone), kind=kOutput, calls=%fused_computation.987 | convolution fusion | flops 805306368 | bytes 10485760 | tf_op jit(solution)/shard_map/brn,bkn->brk/dot_general | solution.py:101
  219.0 1.8 copy-done.1
  220.8 1.8 fusion.248
  222.6 3.8 fusion.24
  227.7 5.4 %all-to-all-start.4 = ((f32[32,64,128]{2,1,0:T(8,128)}), f32[32,64,128]{2,1,0:T(8,128)}, u32[]{:S(2)}, u32[]{:S(2)}) async-start(f32[32,64,128]{2,1,0:T(8,128)} %bitcast.2054), calls=%async_computation.4 | async-start | bytes 2097152 | tf_op jit(solution)/shard_map/all_to_all | solution.py:125
  233.1 6.0 %fusion.18 = f32[4,512,128]{2,1,0:T(8,128)S(1)} fusion(f32[4,512,512]{1,2,0:T(8,128)} %constant.101.clone, f32[4,512,128]{2,1,0:T(8,128)S(1)} %fusion.248, f32[4,512]{1,0:T(4,128)S(1)} %copy-done.66, f32[128]{0:T(128)} %dynamic-slice_multiply_fusion), kind=kOutput, calls=%fused_computation.32 | convolution fusion | flops 806354944 | bytes 6300160 | tf_op jit(solution)/shard_map/bkn,bnc->bkc/dot_general | solution.py:117
  244.7 14.7 %all-to-all-done.4 = f32[32,64,128]{2,1,0:T(8,128)} async-done(((f32[32,64,128]{2,1,0:T(8,128)}), f32[32,64,128]{2,1,0:T(8,128)}, u32[]{:S(2)}, u32[]{:S(2)}) %all-to-all-start.4) | async-done | bytes 1048608 | tf_op jit(solution)/shard_map/all_to_all | solution.py:125
  259.3 3.8 all-to-all-start.8
  263.1 2.9 copy.78
  266.0 1.6 reshape.406
  267.6 7.3 %fusion.249 = f32[8,64,512]{2,1,0:T(8,128)S(1)} fusion(f32[8,64,512]{2,1,0:T(8,128)S(1)} %reshape.406, f32[8,512,512]{2,1,0:T(8,128)} %constant.100.clone), kind=kOutput, calls=%fused_computation.981 | convolution fusion | flops 805306368 | bytes 10485760 | tf_op jit(solution)/shard_map/brn,bkn->brk/dot_general | solution.py:101
  275.6 1.6 fusion.230
  278.1 1.6 slice-done.3
  279.7 3.2 fusion.251
  284.2 5.2 %all-to-all-done.8 = f32[32,64,128]{2,1,0:T(8,128)} async-done(((f32[32,64,128]{2,1,0:T(8,128)}), f32[32,64,128]{2,1,0:T(8,128)}, u32[]{:S(2)}, u32[]{:S(2)}) %all-to-all-start.8) | async-done | bytes 1048608 | tf_op jit(solution)/shard_map/all_to_all | solution.py:125
  289.3 3.8 all-to-all-start.6
  293.1 2.9 copy.75
  296.0 1.6 reshape.417
  297.7 7.3 %fusion.254 = f32[8,64,512]{2,1,0:T(8,128)S(1)} fusion(f32[8,64,512]{2,1,0:T(8,128)S(1)} %reshape.417, f32[8,512,512]{2,1,0:T(8,128)} %constant.100.clone), kind=kOutput, calls=%fused_computation.986 | convolution fusion | flops 805306368 | bytes 10485760 | tf_op jit(solution)/shard_map/brn,bkn->brk/dot_general | solution.py:101
  308.0 11.3 %all-to-all-done.6 = f32[32,64,128]{2,1,0:T(8,128)S(1)} async-done(((f32[32,64,128]{2,1,0:T(8,128)}), f32[32,64,128]{2,1,0:T(8,128)S(1)}, u32[]{:S(2)}, u32[]{:S(2)}) %all-to-all-start.6) | async-done | bytes 1048608 | tf_op jit(solution)/shard_map/all_to_all | solution.py:125
  319.8 1.8 copy-done.2
  321.5 1.8 multiply_multiply_fusion.2
  323.4 3.5 fusion.252
  332.5 3.8 all-to-all-start.7
  338.5 1.5 constant_dynamic-update-slice_fusion.157
  340.0 1.5 constant_dynamic-update-slice_fusion.156
  344.9 17.6 %all-to-all-done.7 = f32[32,64,128]{2,1,0:T(8,128)S(1)} async-done(((f32[32,64,128]{2,1,0:T(8,128)}), f32[32,64,128]{2,1,0:T(8,128)S(1)}, u32[]{:S(2)}, u32[]{:S(2)}) %all-to-all-start.7) | async-done | bytes 1048608 | tf_op jit(solution)/shard_map/all_to_all | solution.py:125
  363.7 7.3 %fusion.253 = f32[8,64,512]{2,1,0:T(8,128)S(1)} fusion(f32[8,64,512]{2,1,0:T(8,128)S(1)} %reshape.414, f32[8,512,512]{2,1,0:T(8,128)} %constant.100.clone), kind=kOutput, calls=%fused_computation.985 | convolution fusion | flops 805306368 | bytes 10485760 | tf_op jit(solution)/shard_map/brn,bkn->brk/dot_general | solution.py:101
  372.9 3.3 fusion.29
  376.2 3.8 all-to-all-start.10
  380.3 4.9 %select_reduce_fusion.1 = f32[2048]{0:T(1024)S(1)} fusion(s32[2048]{0:T(1024)S(1)} %copy-done.89, pred[2048]{0:T(1024)(128)(4,1)S(1)} %lt.37, f32[512,512]{1,0:T(8,128)} %param.11, s32[2048]{0:T(1024)S(1)} %copy-done.88), kind=kOutput, calls=%fused_computation.1 | convolution fusion | flops 3226466304 | bytes 1075200 | tf_op jit(solution)/shard_map/dot_general | solution.py:236
  385.2 10.3 %all-to-all-done.10 = f32[8,64,512]{2,1,0:T(8,128)S(1)} async-done(((f32[8,64,512]{2,1,0:T(8,128)}), f32[8,64,512]{2,1,0:T(8,128)S(1)}, u32[]{:S(2)}, u32[]{:S(2)}) %all-to-all-start.10) | async-done | bytes 1048608 | tf_op jit(solution)/shard_map/all_to_all | solution.py:219
  395.5 3.7 select_reduce_fusion
  399.8 3.6 all-to-all-start.11
  404.2 3.9 all-to-all-done.11
  408.1 1.8 fusion.3
  413.1 3.0 collective-permute-start.5
  417.4 4.5 %collective-permute-start.7 = (f32[3,16,1,128]{3,2,1,0:T(1,128)S(1)}, f32[3,16,1,128]{3,2,1,0:T(1,128)S(1)}, u32[]{:S(2)}, u32[]{:S(2)}) collective-permute-start(f32[3,16,1,128]{3,2,1,0:T(1,128)S(1)} %get-tuple-element.348), channel_id=1, source_target_pairs={{0,1},{1,2},{2,3},{4,5},{5,6},{6,7},{8,9},{9,10},{10,11},{12,13},{... | collective-permute-start | bytes 73736 | tf_op jit(solution)/shard_map/ppermute | solution.py:143
  (478 shorter events, 86.2 us)
Async XLA Ops:
  41.4 18.1 %copy-start.90 = (s32[1,1,8,256]{3,2,1,0:T(8,128)S(1)}, s32[1,1,8,256]{3,2,1,0:T(8,128)}, u32[]{:S(2)}) copy-start(s32[1,1,8,256]{3,2,1,0:T(8,128)} %param.14) | copy-start | bytes 24580
  41.4 18.1 %copy-start.74 = (f32[4,16,16]{2,1,0:T(8,128)S(1)}, f32[4,16,16]{2,1,0:T(8,128)}, u32[]{:S(2)}) copy-start(f32[4,16,16]{2,1,0:T(8,128)} %param.17) | copy-start | bytes 12292
  41.5 21.4 %copy-start.76 = (s32[4,16,16]{2,1,0:T(8,128)S(1)}, s32[4,16,16]{2,1,0:T(8,128)}, u32[]{:S(2)}) copy-start(s32[4,16,16]{2,1,0:T(8,128)} %param.16) | copy-start | bytes 12292
  42.6 30.5 %all-to-all-start.1 = ((f32[32,64,128]{2,1,0:T(8,128)}), f32[32,64,128]{2,1,0:T(8,128)S(1)}, u32[]{:S(2)}, u32[]{:S(2)}) async-start(f32[32,64,128]{2,1,0:T(8,128)} %bitcast.11), calls=%async_computation.1 | async-start | bytes 2097152 | tf_op jit(solution)/shard_map/all_to_all | solution.py:125
  47.3 363.0 %collective-permute-start = (f32[3,1,16,128]{3,2,1,0:T(8,128)}, f32[3,1,16,128]{3,2,1,0:T(8,128)}, u32[]{:S(2)}, u32[]{:S(2)}) collective-permute-start(f32[3,1,16,128]{3,2,1,0:T(8,128)} %get-tuple-element.354), channel_id=1, source_target_pairs={{4,0},{8,4},{12,8},{16,12},{20,16},{24,20},{28,24},{5,1},{9,5},{13... | collective-permute-start | bytes 73736 | tf_op jit(solution)/shard_map/ppermute | solution.py:144
  48.5 361.7 %collective-permute-start.1 = (f32[3,1,16,128]{3,2,1,0:T(8,128)}, f32[3,1,16,128]{3,2,1,0:T(8,128)}, u32[]{:S(2)}, u32[]{:S(2)}) collective-permute-start(f32[3,1,16,128]{3,2,1,0:T(8,128)} %get-tuple-element.355), channel_id=1, source_target_pairs={{0,4},{4,8},{8,12},{12,16},{16,20},{20,24},{24,28},{1,5},{5,9},{9,... | collective-permute-start | bytes 73736 | tf_op jit(solution)/shard_map/ppermute | solution.py:143
  52.8 357.4 %collective-permute-start.2 = (f32[3,16,1,128]{3,2,1,0:T(1,128)}, f32[3,16,1,128]{3,2,1,0:T(1,128)}, u32[]{:S(2)}, u32[]{:S(2)}) collective-permute-start(f32[3,16,1,128]{3,2,1,0:T(1,128)} %get-tuple-element.358), channel_id=1, source_target_pairs={{1,0},{2,1},{3,2},{5,4},{6,5},{7,6},{9,8},{10,9},{11,10},{13,12},{... | collective-permute-start | bytes 73736 | tf_op jit(solution)/shard_map/ppermute | solution.py:144
  54.1 356.1 %collective-permute-start.3 = (f32[3,16,1,128]{3,2,1,0:T(1,128)}, f32[3,16,1,128]{3,2,1,0:T(1,128)}, u32[]{:S(2)}, u32[]{:S(2)}) collective-permute-start(f32[3,16,1,128]{3,2,1,0:T(1,128)} %get-tuple-element.359), channel_id=1, source_target_pairs={{0,1},{1,2},{2,3},{4,5},{5,6},{6,7},{8,9},{9,10},{10,11},{12,13},{... | collective-permute-start | bytes 73736 | tf_op jit(solution)/shard_map/ppermute | solution.py:143
  91.7 29.8 %all-to-all-start.2 = ((f32[32,64,128]{2,1,0:T(8,128)}), f32[32,64,128]{2,1,0:T(8,128)}, u32[]{:S(2)}, u32[]{:S(2)}) async-start(f32[32,64,128]{2,1,0:T(8,128)} %bitcast.2053), calls=%async_computation.2 | async-start | bytes 2097152 | tf_op jit(solution)/shard_map/all_to_all | solution.py:125
  121.5 30.0 %all-to-all-start.5 = ((f32[32,64,128]{2,1,0:T(8,128)}), f32[32,64,128]{2,1,0:T(8,128)}, u32[]{:S(2)}, u32[]{:S(2)}) async-start(f32[32,64,128]{2,1,0:T(8,128)} %bitcast.2052), calls=%async_computation.5 | async-start | bytes 2097152 | tf_op jit(solution)/shard_map/all_to_all | solution.py:125
  151.4 34.8 %all-to-all-start.9 = ((f32[32,64,128]{2,1,0:T(8,128)}), f32[32,64,128]{2,1,0:T(8,128)}, u32[]{:S(2)}, u32[]{:S(2)}) async-start(f32[32,64,128]{2,1,0:T(8,128)} %bitcast.201), calls=%async_computation.9 | async-start | bytes 2097152 | tf_op jit(solution)/shard_map/all_to_all | solution.py:125
  160.9 9.2 %copy-start.55 = (f32[64,256]{1,0:T(8,128)S(1)}, f32[64,256]{1,0:T(8,128)}, u32[]{:S(2)}) copy-start(f32[64,256]{1,0:T(8,128)} %get-tuple-element.169) | copy-start | bytes 196612
  160.9 9.2 %copy-start.56 = (f32[64,256]{1,0:T(8,128)S(1)}, f32[64,256]{1,0:T(8,128)}, u32[]{:S(2)}) copy-start(f32[64,256]{1,0:T(8,128)} %get-tuple-element.170) | copy-start | bytes 196612
  160.9 9.2 %copy-start.57 = (f32[64,256]{1,0:T(8,128)S(1)}, f32[64,256]{1,0:T(8,128)}, u32[]{:S(2)}) copy-start(f32[64,256]{1,0:T(8,128)} %get-tuple-element.171) | copy-start | bytes 196612
  160.9 9.2 %copy-start.58 = (f32[64,256]{1,0:T(8,128)S(1)}, f32[64,256]{1,0:T(8,128)}, u32[]{:S(2)}) copy-start(f32[64,256]{1,0:T(8,128)} %get-tuple-element.172) | copy-start | bytes 196612
  160.9 9.3 %copy-start.59 = (f32[64,256]{1,0:T(8,128)S(1)}, f32[64,256]{1,0:T(8,128)}, u32[]{:S(2)}) copy-start(f32[64,256]{1,0:T(8,128)} %get-tuple-element.166) | copy-start | bytes 196612
  160.9 9.3 %copy-start.60 = (f32[64,256]{1,0:T(8,128)S(1)}, f32[64,256]{1,0:T(8,128)}, u32[]{:S(2)}) copy-start(f32[64,256]{1,0:T(8,128)} %get-tuple-element.167) | copy-start | bytes 196612
  177.7 7.8 %copy-start.51 = (f32[64,256]{1,0:T(8,128)}, f32[64,256]{1,0:T(8,128)S(1)}, u32[]{:S(2)}) copy-start(f32[64,256]{1,0:T(8,128)S(1)} %get-tuple-element.109) | copy-start | bytes 196612
  177.7 7.8 %copy-start.53 = (f32[64,256]{1,0:T(8,128)}, f32[64,256]{1,0:T(8,128)S(1)}, u32[]{:S(2)}) copy-start(f32[64,256]{1,0:T(8,128)S(1)} %get-tuple-element.110) | copy-start | bytes 196612
  178.4 7.1 %copy-start.49 = (f32[64,256]{1,0:T(8,128)}, f32[64,256]{1,0:T(8,128)S(1)}, u32[]{:S(2)}) copy-start(f32[64,256]{1,0:T(8,128)S(1)} %get-tuple-element.104) | copy-start | bytes 196612
  186.2 32.4 %all-to-all-start.3 = ((f32[32,64,128]{2,1,0:T(8,128)}), f32[32,64,128]{2,1,0:T(8,128)S(1)}, u32[]{:S(2)}, u32[]{:S(2)}) async-start(f32[32,64,128]{2,1,0:T(8,128)} %bitcast.2041), calls=%async_computation.3 | async-start | bytes 2097152 | tf_op jit(solution)/shard_map/all_to_all | solution.py:125
  197.9 9.1 %copy-start.52 = (f32[64,256]{1,0:T(8,128)S(1)}, f32[64,256]{1,0:T(8,128)}, u32[]{:S(2)}) copy-start(f32[64,256]{1,0:T(8,128)} %copy-done.51) | copy-start | bytes 196612
  197.9 9.1 %copy-start.54 = (f32[64,256]{1,0:T(8,128)S(1)}, f32[64,256]{1,0:T(8,128)}, u32[]{:S(2)}) copy-start(f32[64,256]{1,0:T(8,128)} %copy-done.53) | copy-start | bytes 196612
  197.9 9.1 %copy-start.73 = (f32[64,256]{1,0:T(8,128)S(1)}, f32[64,256]{1,0:T(8,128)}, u32[]{:S(2)}) copy-start(f32[64,256]{1,0:T(8,128)} %get-tuple-element.101) | copy-start | bytes 196612
  227.7 31.6 %all-to-all-start.4 = ((f32[32,64,128]{2,1,0:T(8,128)}), f32[32,64,128]{2,1,0:T(8,128)}, u32[]{:S(2)}, u32[]{:S(2)}) async-start(f32[32,64,128]{2,1,0:T(8,128)} %bitcast.2054), calls=%async_computation.4 | async-start | bytes 2097152 | tf_op jit(solution)/shard_map/all_to_all | solution.py:125
  259.3 30.0 %all-to-all-start.8 = ((f32[32,64,128]{2,1,0:T(8,128)}), f32[32,64,128]{2,1,0:T(8,128)}, u32[]{:S(2)}, u32[]{:S(2)}) async-start(f32[32,64,128]{2,1,0:T(8,128)} %bitcast.174), calls=%async_computation.8 | async-start | bytes 2097152 | tf_op jit(solution)/shard_map/all_to_all | solution.py:125
  289.3 30.0 %all-to-all-start.6 = ((f32[32,64,128]{2,1,0:T(8,128)}), f32[32,64,128]{2,1,0:T(8,128)S(1)}, u32[]{:S(2)}, u32[]{:S(2)}) async-start(f32[32,64,128]{2,1,0:T(8,128)} %bitcast.129), calls=%async_computation.6 | async-start | bytes 2097152 | tf_op jit(solution)/shard_map/all_to_all | solution.py:125
  308.0 11.4 %copy-start.15 = (f32[64,4096]{1,0:T(8,128)}, f32[64,4096]{1,0:T(8,128)S(1)}, u32[]{:S(2)}) copy-start(f32[64,4096]{1,0:T(8,128)S(1)} %get-tuple-element.132) | copy-start | bytes 3145732
  326.9 9.5 %copy-start.34 = (f32[64,256]{1,0:T(8,128)S(1)}, f32[64,256]{1,0:T(8,128)}, u32[]{:S(2)}) copy-start(f32[64,256]{1,0:T(8,128)} %copy-done.33) | copy-start | bytes 196612
  326.9 9.5 %copy-start.36 = (f32[64,256]{1,0:T(8,128)S(1)}, f32[64,256]{1,0:T(8,128)}, u32[]{:S(2)}) copy-start(f32[64,256]{1,0:T(8,128)} %copy-done.35) | copy-start | bytes 196612
  326.9 9.5 %copy-start.38 = (f32[64,256]{1,0:T(8,128)S(1)}, f32[64,256]{1,0:T(8,128)}, u32[]{:S(2)}) copy-start(f32[64,256]{1,0:T(8,128)} %copy-done.37) | copy-start | bytes 196612
  326.9 9.5 %copy-start.40 = (f32[64,256]{1,0:T(8,128)S(1)}, f32[64,256]{1,0:T(8,128)}, u32[]{:S(2)}) copy-start(f32[64,256]{1,0:T(8,128)} %copy-done.39) | copy-start | bytes 196612
  326.9 9.5 %copy-start.45 = (f32[64,256]{1,0:T(8,128)S(1)}, f32[64,256]{1,0:T(8,128)}, u32[]{:S(2)}) copy-start(f32[64,256]{1,0:T(8,128)} %get-tuple-element.135) | copy-start | bytes 196612
  326.9 9.5 %copy-start.46 = (f32[64,256]{1,0:T(8,128)S(1)}, f32[64,256]{1,0:T(8,128)}, u32[]{:S(2)}) copy-start(f32[64,256]{1,0:T(8,128)} %get-tuple-element.136) | copy-start | bytes 196612
  327.6 9.4 %copy-start.18 = (f32[64,256]{1,0:T(8,128)S(1)}, f32[64,256]{1,0:T(8,128)}, u32[]{:S(2)}) copy-start(f32[64,256]{1,0:T(8,128)} %copy-done.17) | copy-start | bytes 196612
  327.6 9.4 %copy-start.20 = (f32[64,256]{1,0:T(8,128)S(1)}, f32[64,256]{1,0:T(8,128)}, u32[]{:S(2)}) copy-start(f32[64,256]{1,0:T(8,128)} %copy-done.19) | copy-start | bytes 196612
  327.7 9.4 %copy-start.26 = (f32[64,256]{1,0:T(8,128)S(1)}, f32[64,256]{1,0:T(8,128)}, u32[]{:S(2)}) copy-start(f32[64,256]{1,0:T(8,128)} %copy-done.25) | copy-start | bytes 196612
  327.7 9.4 %copy-start.28 = (f32[64,256]{1,0:T(8,128)S(1)}, f32[64,256]{1,0:T(8,128)}, u32[]{:S(2)}) copy-start(f32[64,256]{1,0:T(8,128)} %copy-done.27) | copy-start | bytes 196612
  327.7 10.1 %copy-start.22 = (f32[64,256]{1,0:T(8,128)S(1)}, f32[64,256]{1,0:T(8,128)}, u32[]{:S(2)}) copy-start(f32[64,256]{1,0:T(8,128)} %copy-done.21) | copy-start | bytes 196612
  327.7 10.1 %copy-start.24 = (f32[64,256]{1,0:T(8,128)S(1)}, f32[64,256]{1,0:T(8,128)}, u32[]{:S(2)}) copy-start(f32[64,256]{1,0:T(8,128)} %copy-done.23) | copy-start | bytes 196612
  327.7 10.8 %copy-start.42 = (f32[64,256]{1,0:T(8,128)S(1)}, f32[64,256]{1,0:T(8,128)}, u32[]{:S(2)}) copy-start(f32[64,256]{1,0:T(8,128)} %copy-done.41) | copy-start | bytes 196612
  327.7 10.8 %copy-start.44 = (f32[64,256]{1,0:T(8,128)S(1)}, f32[64,256]{1,0:T(8,128)}, u32[]{:S(2)}) copy-start(f32[64,256]{1,0:T(8,128)} %copy-done.43) | copy-start | bytes 196612
  328.4 13.1 %copy-start.30 = (f32[64,256]{1,0:T(8,128)S(1)}, f32[64,256]{1,0:T(8,128)}, u32[]{:S(2)}) copy-start(f32[64,256]{1,0:T(8,128)} %copy-done.29) | copy-start | bytes 196612
  328.4 13.1 %copy-start.32 = (f32[64,256]{1,0:T(8,128)S(1)}, f32[64,256]{1,0:T(8,128)}, u32[]{:S(2)}) copy-start(f32[64,256]{1,0:T(8,128)} %copy-done.31) | copy-start | bytes 196612
  332.5 30.1 %all-to-all-start.7 = ((f32[32,64,128]{2,1,0:T(8,128)}), f32[32,64,128]{2,1,0:T(8,128)S(1)}, u32[]{:S(2)}, u32[]{:S(2)}) async-start(f32[32,64,128]{2,1,0:T(8,128)} %bitcast.147), calls=%async_computation.7 | async-start | bytes 2097152 | tf_op jit(solution)/shard_map/all_to_all | solution.py:125
  372.9 7.1 %copy-start.91 = (s32[1,1,8]{2,1,0:T(1,128)S(1)}, s32[1,1,8]{2,1,0:T(1,128)}, u32[]{:S(2)}) copy-start(s32[1,1,8]{2,1,0:T(1,128)} %param.15) | copy-start | bytes 100
  376.2 19.2 %all-to-all-start.10 = ((f32[8,64,512]{2,1,0:T(8,128)}), f32[8,64,512]{2,1,0:T(8,128)S(1)}, u32[]{:S(2)}, u32[]{:S(2)}) async-start(f32[8,64,512]{2,1,0:T(8,128)} %fusion.29), calls=%async_computation.10 | async-start | bytes 2097152 | tf_op jit(solution)/shard_map/all_to_all | solution.py:219
  395.5 8.0 %copy-start.84 = (f32[1,16,16]{2,1,0:T(8,128)S(1)}, f32[1,16,16]{2,1,0:T(8,128)}, u32[]{:S(2)}) copy-start(f32[1,16,16]{2,1,0:T(8,128)} %get-tuple-element.394) | copy-start | bytes 3076
  395.5 8.1 %copy-start.83 = (f32[1,16,16]{2,1,0:T(8,128)S(1)}, f32[1,16,16]{2,1,0:T(8,128)}, u32[]{:S(2)}) copy-start(f32[1,16,16]{2,1,0:T(8,128)} %get-tuple-element.397) | copy-start | bytes 3076
  395.5 8.2 %copy-start.82 = (f32[1,16,16]{2,1,0:T(8,128)S(1)}, f32[1,16,16]{2,1,0:T(8,128)}, u32[]{:S(2)}) copy-start(f32[1,16,16]{2,1,0:T(8,128)} %get-tuple-element.396) | copy-start | bytes 3076
  395.5 8.2 %copy-start.80 = (f32[1,16,16]{2,1,0:T(8,128)S(1)}, f32[1,16,16]{2,1,0:T(8,128)}, u32[]{:S(2)}) copy-start(f32[1,16,16]{2,1,0:T(8,128)} %get-tuple-element.395) | copy-start | bytes 3076
  395.5 8.3 %copy-start.81 = (s32[1,16,16]{2,1,0:T(8,128)S(1)}, s32[1,16,16]{2,1,0:T(8,128)}, u32[]{:S(2)}) copy-start(s32[1,16,16]{2,1,0:T(8,128)} %get-tuple-element.393) | copy-start | bytes 3076
  395.5 8.4 %copy-start.79 = (s32[1,16,16]{2,1,0:T(8,128)S(1)}, s32[1,16,16]{2,1,0:T(8,128)}, u32[]{:S(2)}) copy-start(s32[1,16,16]{2,1,0:T(8,128)} %get-tuple-element.392) | copy-start | bytes 3076
  395.5 8.5 %copy-start.78 = (s32[1,16,16]{2,1,0:T(8,128)S(1)}, s32[1,16,16]{2,1,0:T(8,128)}, u32[]{:S(2)}) copy-start(s32[1,16,16]{2,1,0:T(8,128)} %get-tuple-element.390) | copy-start | bytes 3076
  395.5 8.6 %copy-start.77 = (s32[1,16,16]{2,1,0:T(8,128)S(1)}, s32[1,16,16]{2,1,0:T(8,128)}, u32[]{:S(2)}) copy-start(s32[1,16,16]{2,1,0:T(8,128)} %get-tuple-element.391) | copy-start | bytes 3076
  399.2 11.1 %copy-start.63 = (f32[16,16,128]{2,1,0:T(8,128)S(1)}, f32[16,16,128]{2,1,0:T(8,128)}, u32[]{:S(2)}) copy-start(f32[16,16,128]{2,1,0:T(8,128)} %get-tuple-element.349) | copy-start | bytes 393220
  399.2 11.1 %copy-start.64 = (f32[16,16,128]{2,1,0:T(8,128)S(1)}, f32[16,16,128]{2,1,0:T(8,128)}, u32[]{:S(2)}) copy-start(f32[16,16,128]{2,1,0:T(8,128)} %get-tuple-element.350) | copy-start | bytes 393220
  399.2 11.1 %copy-start.65 = (f32[16,16,128]{2,1,0:T(8,128)S(1)}, f32[16,16,128]{2,1,0:T(8,128)}, u32[]{:S(2)}) copy-start(f32[16,16,128]{2,1,0:T(8,128)} %get-tuple-element.351) | copy-start | bytes 393220
  399.2 11.1 %copy-start.75 = (f32[16,16]{1,0:T(8,128)S(1)}, f32[16,16]{1,0:T(8,128)}, u32[]{:S(2)}) copy-start(f32[16,16]{1,0:T(8,128)} %get-tuple-element.401) | copy-start | bytes 3076
  399.8 8.3 %all-to-all-start.11 = ((f32[2,8,256]{2,0,1:T(2,128)}), f32[2,8,256]{2,0,1:T(2,128)S(1)}, u32[]{:S(2)}, u32[]{:S(2)}) async-start(f32[2,8,256]{2,0,1:T(2,128)} %pad_maximum_fusion.12), calls=%async_computation.11 | async-start | bytes 32768 | tf_op jit(solution)/shard_map/all_to_all | solution.py:240
  411.8 10.2 %collective-permute-start.4 = (f32[3,1,16,128]{3,2,1,0:T(8,128)S(1)}, f32[3,1,16,128]{3,2,1,0:T(8,128)S(1)}, u32[]{:S(2)}, u32[]{:S(2)}) collective-permute-start(f32[3,1,16,128]{3,2,1,0:T(8,128)S(1)} %get-tuple-element.343), channel_id=1, source_target_pairs={{4,0},{8,4},{12,8},{16,12},{20,16},{24,20},{28,24},{5,1},{9,5},{13... | collective-permute-start | bytes 73736 | tf_op jit(solution)/shard_map/ppermute | solution.py:144
  413.1 8.9 %collective-permute-start.5 = (f32[3,1,16,128]{3,2,1,0:T(8,128)S(1)}, f32[3,1,16,128]{3,2,1,0:T(8,128)S(1)}, u32[]{:S(2)}, u32[]{:S(2)}) collective-permute-start(f32[3,1,16,128]{3,2,1,0:T(8,128)S(1)} %get-tuple-element.344), channel_id=1, source_target_pairs={{0,4},{4,8},{8,12},{12,16},{16,20},{20,24},{24,28},{1,5},{5,9},{9,... | collective-permute-start | bytes 73736 | tf_op jit(solution)/shard_map/ppermute | solution.py:143
  416.1 5.9 %collective-permute-start.6 = (f32[3,16,1,128]{3,2,1,0:T(1,128)S(1)}, f32[3,16,1,128]{3,2,1,0:T(1,128)S(1)}, u32[]{:S(2)}, u32[]{:S(2)}) collective-permute-start(f32[3,16,1,128]{3,2,1,0:T(1,128)S(1)} %get-tuple-element.347), channel_id=1, source_target_pairs={{1,0},{2,1},{3,2},{5,4},{6,5},{7,6},{9,8},{10,9},{11,10},{13,12},{... | collective-permute-start | bytes 73736 | tf_op jit(solution)/shard_map/ppermute | solution.py:144
  417.4 6.1 %collective-permute-start.7 = (f32[3,16,1,128]{3,2,1,0:T(1,128)S(1)}, f32[3,16,1,128]{3,2,1,0:T(1,128)S(1)}, u32[]{:S(2)}, u32[]{:S(2)}) collective-permute-start(f32[3,16,1,128]{3,2,1,0:T(1,128)S(1)} %get-tuple-element.348), channel_id=1, source_target_pairs={{0,1},{1,2},{2,3},{4,5},{5,6},{6,7},{8,9},{9,10},{10,11},{12,13},{... | collective-permute-start | bytes 73736 | tf_op jit(solution)/shard_map/ppermute | solution.py:143
  (51 other events, 128.0 us)

commit v2 on v1

--- a/solution.py
+++ b/solution.py
@@ -4,6 +4,8 @@
 import jax.numpy as jnp
 import numpy as np
 from jax import lax
+from jax.experimental import pallas as pl
+from jax.experimental.pallas import tpu as pltpu
 from jax.sharding import PartitionSpec as P
 
 NXW = 4096
@@ -52,9 +54,37 @@
     return tuple(out)
 
 
+def real_dft_transposed(bins):
+    half = len(bins) - 1
+    size = 2 * half
+    if size == 2:
+        return [bins[0][0] + bins[1][0], bins[0][0] - bins[1][0]]
+    even, odd = [None] * (half // 2 + 1), [None] * (half // 2 + 1)
+    for k in range(size // 4 + 1):
+        re, im = bins[k]
+        if k == 0:
+            even[0] = (re + bins[half][0], None)
+            odd[0] = (re - bins[half][0], None)
+        elif 4 * k == size:
+            even[k] = (re, None)
+            odd[k] = (-im, None)
+        else:
+            other_re, other_im = bins[half - k]
+            c, s = math.cos(2.0 * math.pi * k / size), math.sin(2.0 * math.pi * k / size)
+            turned_re, turned_im = re - other_re, im + other_im
+            even[k] = (re + other_re, im - other_im)
+            odd[k] = (c * turned_re - s * turned_im, s * turned_re + c * turned_im)
+    result = [None] * size
+    result[0::2] = real_dft_transposed(even)
+    result[1::2] = real_dft_transposed(odd)
+    return result
+
+
 def outer_dft_transposed(pieces):
-    shapes = tuple(jax.ShapeDtypeStruct(piece.shape, piece.dtype) for piece in pieces)
-    return jax.linear_transpose(lambda *parts: outer_dft(parts), *shapes)(tuple(pieces))
+    half = len(pieces) // 2
+    bins = [(pieces[0], None)]
+    bins += [(pieces[2 * k], pieces[2 * k + 1]) for k in range(1, half)]
+    return real_dft_transposed(bins + [(pieces[1], None)])
 
 
 def tables(length):
@@ -125,67 +155,368 @@
     return lax.all_to_all(values, BOTH, split_axis=0, concat_axis=0, tiled=True)
 
 
-def ramp_weight(distance, reach_len):
-    ratio = jnp.clip(1.0 - distance / reach_len, 0.0, 1.0)
-    return ratio * ratio
-
-
-def blend_weight(pos_x, pos_y, total_x, total_y, reach_x, reach_y):
-    along_x = jnp.maximum(ramp_weight(pos_x, reach_x), ramp_weight(total_x - 1.0 - pos_x, reach_x))
-    across = jnp.maximum(ramp_weight(pos_y, reach_y), ramp_weight(total_y - 1.0 - pos_y, reach_y))
-    return jnp.maximum(along_x[:, None], across[None, :])[:, :, None]
-
-
-def neighbours(shard, axis, dim):
-    size, length = lax.axis_size(axis), shard.shape[dim]
-    up = [(i, i + 1) for i in range(size - 1)]
-    down = [(i + 1, i) for i in range(size - 1)]
-    before = lax.ppermute(lax.slice_in_dim(shard, length - 1, length, axis=dim), axis, up)
-    after = lax.ppermute(lax.slice_in_dim(shard, 0, 1, axis=dim), axis, down)
-    minus = jnp.concatenate([before, lax.slice_in_dim(shard, 0, length - 1, axis=dim)], axis=dim)
-    plus = jnp.concatenate([lax.slice_in_dim(shard, 1, length, axis=dim), after], axis=dim)
-    return minus, plus
-
-
-def predict(velocity):
-    minus_x, plus_x = neighbours(velocity, "slab", 1)
-    minus_y, plus_y = neighbours(velocity, "pencil", 2)
-    padded = jnp.pad(velocity, ((0, 0), (0, 0), (0, 0), (1, 1)))
-    minus_z, plus_z = padded[..., :-2], padded[..., 2:]
-    laplace = plus_x + minus_x + (plus_y + minus_y) + (plus_z + minus_z) - 6.0 * velocity
-    advect = (
-        velocity[0] * (plus_x - minus_x)
-        + velocity[1] * (plus_y - minus_y)
-        + velocity[2] * (plus_z - minus_z)
-    )
-    return velocity + TIME_STEP * (VISCOSITY * laplace - 0.5 * advect)
-
-
-def on_device(
-    surface_eta, surface_potential, velocity, send_point, send_count, stencil, interp_weight
+def split(values):
+    high = values.astype(jnp.bfloat16)
+    return high, (values - high.astype(jnp.float32)).astype(jnp.bfloat16)
+
+
+def row_product(values, high_ref, low_ref, block, contract):
+    rows = values.shape[0]
+    high, low = split(values)
+    dims = (((1,), (contract,)), ((), ()))
+    main = lax.dot_general(
+        jnp.concatenate([high, low], axis=0),
+        high_ref[block],
+        dims,
+        preferred_element_type=jnp.float32,
+    )
+    rest = lax.dot_general(high, low_ref[block], dims, preferred_element_type=jnp.float32)
+    return main[:rows] + (main[rows:] + rest)
+
+
+def column_product(values, high_ref, low_ref, block):
+    columns = values.shape[1]
+    high, low = split(values)
+    main = jnp.dot(
+        high_ref[block],
+        jnp.concatenate([high, low], axis=1),
+        preferred_element_type=jnp.float32,
+    )
+    rest = jnp.dot(low_ref[block], high, preferred_element_type=jnp.float32)
+    return main[:, :columns] + (main[:, columns:] + rest)
+
+
+def surface_kernel(
+    slab_count,
+    pencil_count,
+    potential_ref,
+    eta_ref,
+    magnitude_ref,
+    row_high_in,
+    row_low_in,
+    col_high_in,
+    col_low_in,
+    colt_high_in,
+    colt_low_in,
+    out_ref,
+    row_high,
+    row_low,
+    col_high,
+    col_low,
+    colt_high,
+    colt_low,
+    potential,
+    eta,
+    back,
+    total,
+    curve,
+    stage_rows,
+    stage_cols,
+    spectrum,
+    sent,
+    held,
+    table_sem,
+    send_sem,
+    recv_sem,
 ):
-    slab_count = lax.axis_size("slab")
-    pencil_count = lax.axis_size("pencil")
+    slab = lax.axis_index("slab")
+    pencil = lax.axis_index("pencil")
     device_count = slab_count * pencil_count
-    slab_index = lax.axis_index("slab")
-    pencil_index = lax.axis_index("pencil")
-    tile_rows, tile_cols = surface_eta.shape
+    own = pencil * slab_count + slab
+    rows = sent.shape[2]
+    columns = sent.shape[3]
+    per_block = 2 * INNER // columns
+    row_blocks = row_high.shape[0]
+    col_blocks = col_high.shape[0]
+    chunk = potential.shape[2]
+    per_part = INNER // rows
+    row_parts = 2 * row_blocks
+    col_parts = 2 * col_blocks
+    step = 8
+
+    pairs = (
+        (row_high_in, row_high),
+        (row_low_in, row_low),
+        (colt_high_in, colt_high),
+        (colt_low_in, colt_low),
+        (col_high_in, col_high),
+        (col_low_in, col_low),
+    )
+    tables_in = [
+        pltpu.make_async_copy(source, target, table_sem.at[i])
+        for i, (source, target) in enumerate(pairs)
+    ]
+    for copy in tables_in:
+        copy.start()
+
+    def partner(i):
+        return lax.rem(pencil + lax.rem(i, pencil_count), pencil_count), lax.rem(
+            slab + i // pencil_count, slab_count
+        )
+
+    barrier = pltpu.get_barrier_semaphore()
+
+    @pl.loop(1, device_count)
+    def _(i):
+        to_pencil, to_slab = partner(i)
+        pl.semaphore_signal(
+            barrier,
+            inc=1,
+            device_id={"slab": to_slab, "pencil": to_pencil},
+            device_id_type=pl.DeviceIdType.MESH,
+        )
+
+    pl.semaphore_wait(barrier, device_count - 1)
+
+    def remote(source, target, index, to_slab, to_pencil):
+        return pltpu.make_async_remote_copy(
+            src_ref=source,
+            dst_ref=target,
+            send_sem=send_sem.at[index],
+            recv_sem=recv_sem.at[index],
+            device_id={"slab": to_slab, "pencil": to_pencil},
+            device_id_type=pl.DeviceIdType.MESH,
+        )
+
+    def send(n):
+        @pl.loop(1, device_count)
+        def _(i):
+            to_pencil, to_slab = partner(i)
+            to = to_pencil * slab_count + to_slab
+            remote(sent.at[n, to], held.at[n, own], n, to_slab, to_pencil).start()
+
+        held[n, own] = sent[n, own]
+
+    def all_of(n):
+        others = pl.ds(0, device_count - 1)
+        return remote(sent.at[n, others], held.at[n, others], n, slab, pencil)
+
+    def send_slab(source_of, target, n):
+        for i in range(1, slab_count):
+            to = lax.rem(slab + i, slab_count)
+            remote(source_of(to), target.at[slab], n, to, pencil).start()
+
+    def all_of_slab(target, n):
+        others = target.at[pl.ds(0, slab_count - 1)]
+        return remote(others, others, n, slab, pencil)
+
+    fields = sent.shape[0]
+
+    def tile_rows(ref):
+        return lambda to: ref.at[pl.ds(pl.multiple_of(to * rows, rows), rows)]
+
+    own_rows = pl.ds(pl.multiple_of(slab * rows, rows), rows)
+    send_slab(tile_rows(potential_ref), potential, fields)
+    send_slab(tile_rows(eta_ref), eta, fields + 1)
+    potential[slab] = potential_ref[own_rows]
+    eta[slab] = eta_ref[own_rows]
+
+    def part_of(ref, part, at):
+        start = part * INNER % chunk
+        return ref.at[part * INNER // chunk, at, pl.ds(start, INNER)]
+
+    def piece_of(piece, at):
+        return stage_rows.at[piece // 2, at, pl.ds(piece % 2 * INNER, INNER)]
+
+    def over_rows(body):
+        @pl.loop(0, rows // step)
+        def _(i):
+            body(pl.ds(pl.multiple_of(i * step, step), step))
+
+    def begin_rows(parts, at):
+        for piece, value in enumerate(outer_dft(parts)):
+            piece_of(piece, at)[...] = value
+
+    def finish_rows(n):
+        @pl.loop(0, row_blocks)
+        def _(b):
+            result = row_product(stage_rows[b], row_high, row_low, b, 0)
+            for i in range(per_block):
+                sent[n, b * per_block + i] = result[:, i * columns : (i + 1) * columns]
+
+        send(n)
+
+    def inverse_rows(n, use):
+        all_of(n).wait_recv()
+
+        @pl.loop(0, row_blocks)
+        def _(b):
+            values = jnp.concatenate(
+                [held[n, b * per_block + i] for i in range(per_block)], axis=1
+            )
+            stage_rows[b] = row_product(values, row_high, row_low, b, 1)
+
+        def body(at):
+            use(at, outer_dft_transposed([piece_of(p, at)[...] for p in range(row_parts)]))
+
+        over_rows(body)
+
+    def over_columns(body):
+        @pl.loop(0, 2 * per_part)
+        def _(i):
+            body(i // 2, pl.multiple_of(lax.rem(i, 2) * (rows // 2), rows // 2))
+
+    def forward_columns(n):
+        all_of(n).wait_recv()
+
+        def body(q, start):
+            parts = [held[n, p * per_part + q, pl.ds(start, rows // 2)] for p in range(col_parts)]
+            for piece, value in enumerate(outer_dft(parts)):
+                at = pl.multiple_of(piece % 2 * INNER + q * rows + start, rows // 2)
+                stage_cols[piece // 2, pl.ds(at, rows // 2)] = value
+
+        over_columns(body)
+
+        @pl.loop(0, col_blocks)
+        def _(b):
+            spectrum[b] = column_product(stage_cols[b], colt_high, colt_low, b)
+
+    def inverse_columns(n):
+        @pl.loop(0, col_blocks)
+        def _(b):
+            values = spectrum[b] * magnitude_ref[b]
+            spectrum[b] = values
+            stage_cols[b] = column_product(values, col_high, col_low, b)
+
+        def body(q, start):
+            pieces = []
+            for piece in range(col_parts):
+                at = pl.multiple_of(piece % 2 * INNER + q * rows + start, rows // 2)
+                pieces.append(stage_cols[piece // 2, pl.ds(at, rows // 2)])
+            for p, value in enumerate(outer_dft_transposed(pieces)):
+                sent[n, p * per_part + q, pl.ds(start, rows // 2)] = value * (1.0 / (NXW * NYW))
+
+        over_columns(body)
+        send(n)
+
+    all_of_slab(potential, fields).wait_recv()
+    over_rows(
+        lambda at: begin_rows([part_of(potential, p, at)[...] for p in range(row_parts)], at)
+    )
+    tables_in[0].wait()
+    tables_in[1].wait()
+    finish_rows(0)
+    for copy in tables_in[2:]:
+        copy.wait()
+
+    forward_columns(0)
+    inverse_columns(1)
+    inverse_columns(2)
+    all_of_slab(eta, fields + 1).wait_recv()
+
+    def use_slope_one(at, parts):
+        for p, value in enumerate(parts):
+            part_of(total, p, at)[...] = value
+        begin_rows([-part_of(eta, p, at)[...] * value for p, value in enumerate(parts)], at)
+
+    def use_curve_one(at, parts):
+        for p, value in enumerate(parts):
+            height = part_of(eta, p, at)[...]
+            term = height * value
+            part_of(total, p, at)[...] += term
+            part_of(curve, p, at)[...] = 0.5 * height * term
+
+    def use_cubic_one(at, parts):
+        for p, value in enumerate(parts):
+            height = part_of(eta, p, at)[...]
+            part_of(total, p, at)[...] += 0.5 * height * height * value
+
+    def use_slope_two(at, parts):
+        following = []
+        for p, value in enumerate(parts):
+            part_of(total, p, at)[...] += value
+            following.append(-part_of(eta, p, at)[...] * value - part_of(curve, p, at)[...])
+        begin_rows(following, at)
+
+    def use_curve_two(at, parts):
+        for p, value in enumerate(parts):
+            part_of(total, p, at)[...] += part_of(eta, p, at)[...] * value
+
+    def use_slope_three(at, parts):
+        for p, value in enumerate(parts):
+            part_of(total, p, at)[...] += value
+
+    inverse_columns(3)
+    inverse_rows(1, use_slope_one)
+    finish_rows(4)
+    inverse_rows(2, use_curve_one)
+    inverse_rows(3, use_cubic_one)
+    forward_columns(4)
+    inverse_columns(5)
+    inverse_columns(6)
+    inverse_rows(5, use_slope_two)
+    finish_rows(7)
+    inverse_rows(6, use_curve_two)
+    forward_columns(7)
+    inverse_columns(8)
+    inverse_rows(8, use_slope_three)
+
+    send_slab(lambda to: total.at[to], back, fields + 2)
+    out_ref[own_rows] = total[slab]
+    all_of_slab(back, fields + 2).wait_recv()
+    for i in range(1, slab_count):
+        source = lax.rem(slab + i, slab_count)
+        out_ref[pl.ds(pl.multiple_of(source * rows, rows), rows)] = back[source]
+    for n in range(fields):
+        all_of(n).wait_send()
+    all_of_slab(potential, fields).wait_send()
+    all_of_slab(eta, fields + 1).wait_send()
+    all_of_slab(back, fields + 2).wait_send()
+
+
+def two_terms(table):
+    high = table.astype(jnp.bfloat16)
+    low = (table - high.astype(np.float32)).astype(jnp.bfloat16)
+    return jnp.asarray(high), jnp.asarray(low)
+
+
+def surface_chain(potential, eta, magnitude, slab_count, pencil_count):
+    tile_rows, tile_cols = eta.shape
+    device_count = slab_count * pencil_count
+    rows, columns = NYW // device_count, NXW // device_count
+    row_table, _ = tables(NXW)
+    col_table, _ = tables(NYW)
+    constants = [
+        *two_terms(row_table),
+        *two_terms(col_table),
+        *two_terms(np.ascontiguousarray(col_table.transpose(0, 2, 1))),
+    ]
+    fields = 9
+    strip = pltpu.VMEM((slab_count, rows, tile_cols), jnp.float32)
+    vmem = pl.BlockSpec(memory_space=pltpu.VMEM)
+    return pl.pallas_call(
+        lambda *refs: surface_kernel(slab_count, pencil_count, *refs),
+        out_shape=jax.ShapeDtypeStruct((tile_rows, tile_cols), jnp.float32),
+        in_specs=[vmem] * 3 + [pl.BlockSpec(memory_space=pl.ANY)] * 6,
+        out_specs=vmem,
+        scratch_shapes=[
+            *(pltpu.VMEM(table.shape, jnp.bfloat16) for table in constants),
+            *([strip] * 5),
+            pltpu.VMEM(row_table.shape[:1] + (rows, 2 * INNER), jnp.float32),
+            pltpu.VMEM(magnitude.shape, jnp.float32),
+            pltpu.VMEM(magnitude.shape, jnp.float32),
+            pltpu.VMEM((fields, device_count, rows, columns), jnp.float32),
+            pltpu.VMEM((fields, device_count, rows, columns), jnp.float32),
+            pltpu.SemaphoreType.DMA((6,)),
+            pltpu.SemaphoreType.DMA((fields + 3,)),
+            pltpu.SemaphoreType.DMA((fields + 3,)),
+        ],
+        compiler_params=pltpu.CompilerParams(
+            collective_id=0, has_side_effects=True, vmem_limit_bytes=56 * 1024 * 1024
+        ),
+    )(potential, eta, magnitude, *constants)
+
+
+def surface_plain(potential, eta, magnitude, row_table, column_table, slab_count):
+    tile_rows, tile_cols = eta.shape
+    columns = magnitude.shape[-1]
+    device_count = NXW // columns
     rows = NYW // device_count
-    columns = NXW // device_count
-    row_table, row_order = tables(NXW)
-    column_table, column_order = tables(NYW)
     row_blocks, column_blocks = jnp.asarray(row_table), jnp.asarray(column_table)
-
-    both = jnp.stack([surface_potential, surface_eta]).reshape(2, slab_count, rows, tile_cols)
+    both = jnp.stack([potential, eta]).reshape(2, slab_count, rows, tile_cols)
     both = lax.all_to_all(both, "slab", split_axis=1, concat_axis=1, tiled=True)
     both = both.transpose(0, 2, 1, 3).reshape(2, rows, NXW)
     potential, eta = both[0], both[1]
-
-    own = pencil_index * slab_count + slab_index
-    wave_x = 2.0 * math.pi / NXW * jnp.asarray(row_order.reshape(-1)).astype(jnp.float32)
-    wave_x = lax.dynamic_slice(wave_x, (own * columns,), (columns,))
-    wave_y = 2.0 * math.pi / NYW * jnp.asarray(column_order).astype(jnp.float32)[:, :, None]
-    magnitude = jnp.sqrt(wave_x * wave_x + wave_y * wave_y)
     first_mult = magnitude * (1.0 / (NXW * NYW))
     second_mult = magnitude * first_mult
     third_mult = magnitude * second_mult
@@ -219,6 +550,72 @@
     vertical = lax.all_to_all(vertical, "slab", split_axis=0, concat_axis=0, tiled=True)
     vertical = vertical.reshape(tile_rows, tile_cols)
 
+    return vertical
+
+
+def ramp_weight(distance, reach_len):
+    ratio = jnp.clip(1.0 - distance / reach_len, 0.0, 1.0)
+    return ratio * ratio
+
+
+def blend_weight(pos_x, pos_y, total_x, total_y, reach_x, reach_y):
+    along_x = jnp.maximum(ramp_weight(pos_x, reach_x), ramp_weight(total_x - 1.0 - pos_x, reach_x))
+    across = jnp.maximum(ramp_weight(pos_y, reach_y), ramp_weight(total_y - 1.0 - pos_y, reach_y))
+    return jnp.maximum(along_x[:, None], across[None, :])[:, :, None]
+
+
+def neighbours(shard, axis, dim):
+    size, length = lax.axis_size(axis), shard.shape[dim]
+    up = [(i, i + 1) for i in range(size - 1)]
+    down = [(i + 1, i) for i in range(size - 1)]
+    before = lax.ppermute(lax.slice_in_dim(shard, length - 1, length, axis=dim), axis, up)
+    after = lax.ppermute(lax.slice_in_dim(shard, 0, 1, axis=dim), axis, down)
+    minus = jnp.concatenate([before, lax.slice_in_dim(shard, 0, length - 1, axis=dim)], axis=dim)
+    plus = jnp.concatenate([lax.slice_in_dim(shard, 1, length, axis=dim), after], axis=dim)
+    return minus, plus
+
+
+def predict(velocity):
+    minus_x, plus_x = neighbours(velocity, "slab", 1)
+    minus_y, plus_y = neighbours(velocity, "pencil", 2)
+    padded = jnp.pad(velocity, ((0, 0), (0, 0), (0, 0), (1, 1)))
+    minus_z, plus_z = padded[..., :-2], padded[..., 2:]
+    laplace = plus_x + minus_x + (plus_y + minus_y) + (plus_z + minus_z) - 6.0 * velocity
+    advect = (
+        velocity[0] * (plus_x - minus_x)
+        + velocity[1] * (plus_y - minus_y)
+        + velocity[2] * (plus_z - minus_z)
+    )
+    return velocity + TIME_STEP * (VISCOSITY * laplace - 0.5 * advect)
+
+
+def on_device(
+    surface_eta, surface_potential, velocity, send_point, send_count, stencil, interp_weight
+):
+    slab_count = lax.axis_size("slab")
+    pencil_count = lax.axis_size("pencil")
+    device_count = slab_count * pencil_count
+    slab_index = lax.axis_index("slab")
+    pencil_index = lax.axis_index("pencil")
+    tile_rows, tile_cols = surface_eta.shape
+    rows = NYW // device_count
+    columns = NXW // device_count
+    own = pencil_index * slab_count + slab_index
+    row_table, row_order = tables(NXW)
+    column_table, column_order = tables(NYW)
+    wave_x = 2.0 * math.pi / NXW * jnp.asarray(row_order.reshape(-1)).astype(jnp.float32)
+    wave_x = lax.dynamic_slice(wave_x, (own * columns,), (columns,))
+    wave_y = 2.0 * math.pi / NYW * jnp.asarray(column_order).astype(jnp.float32)[:, :, None]
+    magnitude = jnp.sqrt(wave_x * wave_x + wave_y * wave_y)
+    if columns % 128 == 0 and rows % 16 == 0 and INNER % rows == 0:
+        vertical = surface_chain(
+            surface_potential, surface_eta, magnitude, slab_count, pencil_count
+        )
+    else:
+        vertical = surface_plain(
+            surface_potential, surface_eta, magnitude, row_table, column_table, slab_count
+        )
+
     points = send_point[0, 0]
     capacity = points.shape[1]
     counts = send_count[0, 0]

time: 432 us -> 312 us (0.72)
  Pallas kernels: 0 us -> 261 us
  waiting for transfers between devices: 108 us -> 1.46 us
  matrix products: 98.3 us -> 11.6 us
  other arithmetic: 71.7 us -> 6.16 us
  local copies, waits for them, and re-layouts: 45.5 us -> 2.97 us
  starting transfers between devices: 67.3 us -> 25.5 us
  blocking collectives: 31.6 us -> 0 us
    pallas_call x0 -> x1, Pallas kernels: none -> 261 us  [surface_chain(): pl.pallas_call(lambda *refs: surface_kernel(slab_count, pencil_count, *re...]
    all_to_all x10 -> x0, waiting for transfers between devices: 103 us -> none  [the longest x9 92.7 us: exchange(): return lax.all_to_all(values, BOTH, split_axis=0, concat_axis=0, tiled=True)]
    dot_general x18 -> x0, matrix products: 87.9 us -> none  [the longest x6 44.6 us: rows_inverse(): stacked = jnp.einsum('brn,bkn->brk', grouped, blocks, precision=HIGH)]
    unnamed x155 -> x0, other arithmetic: 47.5 us -> none
    all_to_all x10 -> x0, starting transfers between devices: 41.9 us -> none  [the longest x9 38.1 us: exchange(): return lax.all_to_all(values, BOTH, split_axis=0, concat_axis=0, tiled=True)]
    all_to_all x1 -> x0, blocking collectives: 31.6 us -> none  [on_device(): both = lax.all_to_all(both, 'slab', split_axis=1, concat_axis=1, tiled=True)]
    reshape x12 -> x0, local copies, waits for them, and re-layouts: 23.6 us -> none  [the longest x6 14.2 us: rows_inverse(): values.reshape(blocks.shape[0], 2 * INNER // columns, rows, columns)]
    unnamed x217 -> x10, local copies, waits for them, and re-layouts: 16.9 us -> 1.7 us
  transfers between devices with their start and end apart: 19 -> 9, of which waited for: 11 -> 1; matrix products, arithmetic and copies ran while one was open for 44% -> 1% of each run, Pallas kernels for 0% -> 0%
where the time goes in v2:
time: 312 us; the launch traced here: 310 us
  Pallas kernels  261 us (84%)
  starting transfers between devices  25.5 us (8%)
  matrix products  11.6 us (4%)
  other arithmetic  6.16 us (2%)
    pallas_call x1, Pallas kernels, surface_chain(): pl.pallas_call(lambda *refs: surface_kernel(slab_count, pencil_count, *re...  261 us
    ppermute x4, starting transfers between devices, neighbours(): lax.ppermute(lax.slice_in_dim(shard, length - 1, length, axis=dim), axis,...  16 us
    dot_general x2, matrix products, pick(): picked_rows = jnp.dot(row_pick, tile, precision=HIGH)  9.79 us
  transfers between devices with their start and end apart: 9, of which 1 were waited for; matrix products, arithmetic and copies ran while one was open for 1% of the time, Pallas kernels for 0%

profile of v2, /device:TPU:0, one launch (start us, length us, event | category | flops | bytes accessed | tf_op | source)
XLA Modules:
  0.0 310.1 jit_solution(8964951321605300305)
XLA Ops:
  0.6 0.7 copy.17
  1.4 0.7 iota_compare_fusion.16
  2.1 0.8 dynamic-slice_multiply_fusion
  2.9 2.0 add_sqrt_fusion.refs_2_
  4.9 4.9 %select_reduce_fusion.1 = f32[2048]{0:T(1024)S(1)} fusion(s32[2048]{0:T(1024)S(1)} %get-tuple-element.35, pred[2048]{0:T(1024)(128)(4,1)S(1)} %lt.37, f32[512,512]{1,0:T(8,128)} %refs_1_.1, s32[2048]{0:T(1024)S(1)} %get-tuple-element.34), kind=kOutput, calls=%fused_computation.1 | convolution fusion | flops 3226466304 | bytes 1075200 | tf_op jit(solution)/shard_map/dot_general | solution.py:633
  9.7 261.4 %shard_map.158 = f32[512,512]{1,0:T(8,128)} custom-call(f32[512,512]{1,0:T(8,128)} %refs_0_.1, f32[512,512]{1,0:T(8,128)} %refs_1_.1, f32[4,512,128]{2,1,0:T(8,128)} %add_sqrt_fusion.refs_2_, bf16[8,512,512]{2,1,0:T(8,128)(2,1)} %constant.100.clone.refs_3_, bf16[8,512,512]{2,1,0:T(8,128)(2,1)} %constant.101.clone.refs_4_, ...), custom_call_target="tpu_custom_call" | custom-call | tf_op jit(solution)/shard_map/pallas_call | solution.py:487
  271.2 0.0 copy-start
  271.2 4.9 %select_reduce_fusion = f32[2048]{0:T(1024)S(1)} fusion(s32[2048]{0:T(1024)S(1)} %get-tuple-element.35, pred[2048]{0:T(1024)(128)(4,1)S(1)} %lt.37, f32[512,512]{1,0:T(8,128)} %shard_map.158, s32[2048]{0:T(1024)S(1)} %get-tuple-element.34), kind=kOutput, calls=%fused_computation | convolution fusion | flops 3226466304 | bytes 1075200 | tf_op jit(solution)/shard_map/dot_general | solution.py:633
  276.1 0.0 copy-start.2
  276.1 0.6 pad_maximum_fusion.8
  276.8 4.2 %all-to-all-start = ((f32[2,8,256]{2,0,1:T(2,128)}), f32[2,8,256]{2,0,1:T(2,128)S(1)}, u32[]{:S(2)}, u32[]{:S(2)}) async-start(f32[2,8,256]{2,0,1:T(2,128)} %pad_maximum_fusion.8), calls=%async_computation | async-start | bytes 32768 | tf_op jit(solution)/shard_map/all_to_all | solution.py:637
  281.0 0.0 copy-done
  281.0 0.0 copy-start.3
  281.0 1.3 collective-permute-start
  282.3 3.0 collective-permute-start.1
  285.4 1.3 collective-permute-start.2
  286.7 4.7 %collective-permute-start.3 = (f32[3,16,1,128]{3,2,1,0:T(1,128)S(1)}, f32[3,16,1,128]{3,2,1,0:T(1,128)S(1)}, u32[]{:S(2)}, u32[]{:S(2)}) collective-permute-start(f32[3,16,1,128]{3,2,1,0:T(1,128)S(1)} %get-tuple-element.25), channel_id=1, source_target_pairs={{0,1},{1,2},{2,3},{4,5},{5,6},{6,7},{8,9},{9,10},{10,11},{12,13},{... | collective-permute-start | bytes 73736 | tf_op jit(solution)/shard_map/ppermute | solution.py:571
  291.5 0.1 fusion.31
  291.5 0.1 fusion.29
  291.6 0.0 copy-done.2
  291.7 0.0 copy-done.3
  291.7 0.1 broadcast_subtract_fusion
  291.8 0.1 broadcast_in_dim.60
  291.9 0.1 broadcast_in_dim.63
  291.9 0.1 broadcast_in_dim.65
  292.0 0.1 broadcast_in_dim.67
  292.1 0.1 eq.103
  292.2 0.1 eq.107
  292.3 0.1 eq.95
  292.3 0.1 eq.99
  292.4 0.1 pad.18.clone
  292.5 0.0 all-to-all-done
  292.5 1.8 fusion.3
  294.3 0.1 mul.247
  294.4 0.1 mul.251
  294.5 0.1 broadcast_multiply_fusion.1
  294.6 0.0 collective-permute-done
  294.6 0.0 collective-permute-done.1
  294.6 0.0 collective-permute-done.2
  294.7 0.0 collective-permute-done.3
  294.7 0.5 multiply_add_fusion.1
  295.2 0.1 fusion.27
  295.2 0.1 fusion.25
  295.3 0.0 copy-start.1
  295.4 1.4 collective-permute-start.4
  296.8 3.7 %collective-permute-start.5 = (f32[3,1,16,128]{3,2,1,0:T(8,128)S(1)}, f32[3,1,16,128]{3,2,1,0:T(8,128)S(1)}, u32[]{:S(2)}, u32[]{:S(2)}) collective-permute-start(f32[3,1,16,128]{3,2,1,0:T(8,128)S(1)} %get-tuple-element.10), channel_id=1, source_target_pairs={{0,4},{4,8},{8,12},{12,16},{16,20},{20,24},{24,28},{1,5},{5,9},{9,... | collective-permute-start | bytes 73736 | tf_op jit(solution)/shard_map/ppermute | solution.py:571
  300.5 1.3 collective-permute-start.6
  301.8 4.5 %collective-permute-start.7 = (f32[3,16,1,128]{3,2,1,0:T(1,128)S(1)}, f32[3,16,1,128]{3,2,1,0:T(1,128)S(1)}, u32[]{:S(2)}, u32[]{:S(2)}) collective-permute-start(f32[3,16,1,128]{3,2,1,0:T(1,128)S(1)} %get-tuple-element.14), channel_id=1, source_target_pairs={{0,1},{1,2},{2,3},{4,5},{5,6},{6,7},{8,9},{9,10},{10,11},{12,13},{... | collective-permute-start | bytes 73736 | tf_op jit(solution)/shard_map/ppermute | solution.py:571
  306.4 0.0 collective-permute-done.4
  306.4 0.0 collective-permute-done.5
  306.4 0.0 collective-permute-done.6
  306.4 1.4 collective-permute-done.7
  307.9 1.3 multiply_add_fusion
  309.1 0.0 copy-done.1
  309.1 1.0 copy.19
  (15 shorter events, 0.2 us)
Async XLA Ops:
  271.2 9.8 %copy-start = (f32[3,16,16,128]{3,2,1,0:T(8,128)S(1)}, f32[3,16,16,128]{3,2,1,0:T(8,128)}, u32[]{:S(2)}) copy-start(f32[3,16,16,128]{3,2,1,0:T(8,128)} %param.17) | copy-start | bytes 1179652
  276.1 15.5 %copy-start.2 = (f32[4,16,16]{2,1,0:T(8,128)S(1)}, f32[4,16,16]{2,1,0:T(8,128)}, u32[]{:S(2)}) copy-start(f32[4,16,16]{2,1,0:T(8,128)} %param.21) | copy-start | bytes 12292
  276.8 15.8 %all-to-all-start = ((f32[2,8,256]{2,0,1:T(2,128)}), f32[2,8,256]{2,0,1:T(2,128)S(1)}, u32[]{:S(2)}, u32[]{:S(2)}) async-start(f32[2,8,256]{2,0,1:T(2,128)} %pad_maximum_fusion.8), calls=%async_computation | async-start | bytes 32768 | tf_op jit(solution)/shard_map/all_to_all | solution.py:637
  281.0 10.7 %copy-start.3 = (s32[4,16,16]{2,1,0:T(8,128)S(1)}, s32[4,16,16]{2,1,0:T(8,128)}, u32[]{:S(2)}) copy-start(s32[4,16,16]{2,1,0:T(8,128)} %param.20) | copy-start | bytes 12292
  281.0 13.6 %collective-permute-start = (f32[3,1,16,128]{3,2,1,0:T(8,128)S(1)}, f32[3,1,16,128]{3,2,1,0:T(8,128)S(1)}, u32[]{:S(2)}, u32[]{:S(2)}) collective-permute-start(f32[3,1,16,128]{3,2,1,0:T(8,128)S(1)} %get-tuple-element.20), channel_id=1, source_target_pairs={{4,0},{8,4},{12,8},{16,12},{20,16},{24,20},{28,24},{5,1},{9,5},{13... | collective-permute-start | bytes 73736 | tf_op jit(solution)/shard_map/ppermute | solution.py:572
  282.3 12.3 %collective-permute-start.1 = (f32[3,1,16,128]{3,2,1,0:T(8,128)S(1)}, f32[3,1,16,128]{3,2,1,0:T(8,128)S(1)}, u32[]{:S(2)}, u32[]{:S(2)}) collective-permute-start(f32[3,1,16,128]{3,2,1,0:T(8,128)S(1)} %get-tuple-element.21), channel_id=1, source_target_pairs={{0,4},{4,8},{8,12},{12,16},{16,20},{20,24},{24,28},{1,5},{5,9},{9,... | collective-permute-start | bytes 73736 | tf_op jit(solution)/shard_map/ppermute | solution.py:571
  285.4 9.2 %collective-permute-start.2 = (f32[3,16,1,128]{3,2,1,0:T(1,128)S(1)}, f32[3,16,1,128]{3,2,1,0:T(1,128)S(1)}, u32[]{:S(2)}, u32[]{:S(2)}) collective-permute-start(f32[3,16,1,128]{3,2,1,0:T(1,128)S(1)} %get-tuple-element.24), channel_id=1, source_target_pairs={{1,0},{2,1},{3,2},{5,4},{6,5},{7,6},{9,8},{10,9},{11,10},{13,12},{... | collective-permute-start | bytes 73736 | tf_op jit(solution)/shard_map/ppermute | solution.py:572
  286.7 8.0 %collective-permute-start.3 = (f32[3,16,1,128]{3,2,1,0:T(1,128)S(1)}, f32[3,16,1,128]{3,2,1,0:T(1,128)S(1)}, u32[]{:S(2)}, u32[]{:S(2)}) collective-permute-start(f32[3,16,1,128]{3,2,1,0:T(1,128)S(1)} %get-tuple-element.25), channel_id=1, source_target_pairs={{0,1},{1,2},{2,3},{4,5},{5,6},{6,7},{8,9},{9,10},{10,11},{12,13},{... | collective-permute-start | bytes 73736 | tf_op jit(solution)/shard_map/ppermute | solution.py:571
  295.3 13.8 %copy-start.1 = (f32[512,512]{1,0:T(8,128)S(1)}, f32[512,512]{1,0:T(8,128)}, u32[]{:S(2)}) copy-start(f32[512,512]{1,0:T(8,128)} %shard_map.158) | copy-start | bytes 3145732
  295.4 11.0 %collective-permute-start.4 = (f32[3,1,16,128]{3,2,1,0:T(8,128)S(1)}, f32[3,1,16,128]{3,2,1,0:T(8,128)S(1)}, u32[]{:S(2)}, u32[]{:S(2)}) collective-permute-start(f32[3,1,16,128]{3,2,1,0:T(8,128)S(1)} %get-tuple-element.9), channel_id=1, source_target_pairs={{4,0},{8,4},{12,8},{16,12},{20,16},{24,20},{28,24},{5,1},{9,5},{13... | collective-permute-start | bytes 73736 | tf_op jit(solution)/shard_map/ppermute | solution.py:572
  296.8 9.6 %collective-permute-start.5 = (f32[3,1,16,128]{3,2,1,0:T(8,128)S(1)}, f32[3,1,16,128]{3,2,1,0:T(8,128)S(1)}, u32[]{:S(2)}, u32[]{:S(2)}) collective-permute-start(f32[3,1,16,128]{3,2,1,0:T(8,128)S(1)} %get-tuple-element.10), channel_id=1, source_target_pairs={{0,4},{4,8},{8,12},{12,16},{16,20},{20,24},{24,28},{1,5},{5,9},{9,... | collective-permute-start | bytes 73736 | tf_op jit(solution)/shard_map/ppermute | solution.py:571
  300.5 5.9 %collective-permute-start.6 = (f32[3,16,1,128]{3,2,1,0:T(1,128)S(1)}, f32[3,16,1,128]{3,2,1,0:T(1,128)S(1)}, u32[]{:S(2)}, u32[]{:S(2)}) collective-permute-start(f32[3,16,1,128]{3,2,1,0:T(1,128)S(1)} %get-tuple-element.13), channel_id=1, source_target_pairs={{1,0},{2,1},{3,2},{5,4},{6,5},{7,6},{9,8},{10,9},{11,10},{13,12},{... | collective-permute-start | bytes 73736 | tf_op jit(solution)/shard_map/ppermute | solution.py:572
  301.8 6.1 %collective-permute-start.7 = (f32[3,16,1,128]{3,2,1,0:T(1,128)S(1)}, f32[3,16,1,128]{3,2,1,0:T(1,128)S(1)}, u32[]{:S(2)}, u32[]{:S(2)}) collective-permute-start(f32[3,16,1,128]{3,2,1,0:T(1,128)S(1)} %get-tuple-element.14), channel_id=1, source_target_pairs={{0,1},{1,2},{2,3},{4,5},{5,6},{6,7},{8,9},{9,10},{10,11},{12,13},{... | collective-permute-start | bytes 73736 | tf_op jit(solution)/shard_map/ppermute | solution.py:571

commit v3 on v2

--- a/solution.py
+++ b/solution.py
@@ -191,7 +191,11 @@
     pencil_count,
     potential_ref,
     eta_ref,
-    magnitude_ref,
+    velocity_ref,
+    row_index_ref,
+    col_index_ref,
+    stencil_ref,
+    share_ref,
     row_high_in,
     row_low_in,
     col_high_in,
@@ -199,6 +203,7 @@
     colt_high_in,
     colt_low_in,
     out_ref,
+    velocity_out,
     row_high,
     row_low,
     col_high,
@@ -213,11 +218,23 @@
     stage_rows,
     stage_cols,
     spectrum,
+    magnitude,
     sent,
     held,
+    tile_split,
+    pick_cols,
+    mix_high,
+    mix_low,
+    picks,
+    arrived,
+    flow,
+    packed,
+    halo,
     table_sem,
     send_sem,
     recv_sem,
+    halo_send,
+    halo_recv,
 ):
     slab = lax.axis_index("slab")
     pencil = lax.axis_index("pencil")
@@ -254,6 +271,7 @@
             slab + i // pencil_count, slab_count
         )
 
+    halo[...] = jnp.zeros(halo.shape, jnp.float32)
     barrier = pltpu.get_barrier_semaphore()
 
     @pl.loop(1, device_count)
@@ -278,14 +296,19 @@
             device_id_type=pl.DeviceIdType.MESH,
         )
 
-    def send(n):
-        @pl.loop(1, device_count)
+    def start(n, to):
+        to_slab, to_pencil = lax.rem(to, slab_count), to // slab_count
+
+        @pl.when(to != own)
+        def _():
+            remote(sent.at[n, to], held.at[n, own], n, to_slab, to_pencil).start()
+
+    def send(n, first, last):
+        @pl.loop(first, last)
         def _(i):
             to_pencil, to_slab = partner(i)
             to = to_pencil * slab_count + to_slab
             remote(sent.at[n, to], held.at[n, own], n, to_slab, to_pencil).start()
-
-        held[n, own] = sent[n, own]
 
     def all_of(n):
         others = pl.ds(0, device_count - 1)
@@ -329,15 +352,18 @@
 
     def finish_rows(n):
         @pl.loop(0, row_blocks)
-        def _(b):
+        def _(i):
+            b = lax.rem(i + own // per_block, row_blocks)
             result = row_product(stage_rows[b], row_high, row_low, b, 0)
             for i in range(per_block):
                 sent[n, b * per_block + i] = result[:, i * columns : (i + 1) * columns]
-
-        send(n)
+                start(n, b * per_block + i)
+
+        held[n, own] = sent[n, own]
 
     def inverse_rows(n, use):
-        all_of(n).wait_recv()
+        if n in (2, 3, 6, 8):
+            all_of(n).wait_recv()
 
         @pl.loop(0, row_blocks)
         def _(b):
@@ -357,7 +383,8 @@
             body(i // 2, pl.multiple_of(lax.rem(i, 2) * (rows // 2), rows // 2))
 
     def forward_columns(n):
-        all_of(n).wait_recv()
+        if n == 0:
+            all_of(n).wait_recv()
 
         def body(q, start):
             parts = [held[n, p * per_part + q, pl.ds(start, rows // 2)] for p in range(col_parts)]
@@ -371,23 +398,228 @@
         def _(b):
             spectrum[b] = column_product(stage_cols[b], colt_high, colt_low, b)
 
-    def inverse_columns(n):
+    def inverse_columns(n, now):
         @pl.loop(0, col_blocks)
         def _(b):
-            values = spectrum[b] * magnitude_ref[b]
+            values = spectrum[b] * magnitude[b]
             spectrum[b] = values
             stage_cols[b] = column_product(values, col_high, col_low, b)
 
-        def body(q, start):
-            pieces = []
-            for piece in range(col_parts):
-                at = pl.multiple_of(piece % 2 * INNER + q * rows + start, rows // 2)
-                pieces.append(stage_cols[piece // 2, pl.ds(at, rows // 2)])
-            for p, value in enumerate(outer_dft_transposed(pieces)):
-                sent[n, p * per_part + q, pl.ds(start, rows // 2)] = value * (1.0 / (NXW * NYW))
-
-        over_columns(body)
-        send(n)
+        @pl.loop(0, per_part)
+        def _(i):
+            q = lax.rem(i + own, per_part)
+            for half in range(2):
+                offset = half * (rows // 2)
+                pieces = []
+                for piece in range(col_parts):
+                    at = pl.multiple_of(piece % 2 * INNER + q * rows + offset, rows // 2)
+                    pieces.append(stage_cols[piece // 2, pl.ds(at, rows // 2)])
+                for p, value in enumerate(outer_dft_transposed(pieces)):
+                    sent[n, p * per_part + q, pl.ds(offset, rows // 2)] = value * (
+                        1.0 / (NXW * NYW)
+                    )
+            if now:
+                for p in range(col_parts):
+                    start(n, p * per_part + q)
+
+        held[n, own] = sent[n, own]
+
+    capacity = row_index_ref.shape[2]
+    block_x, block_y, depth_cells = velocity_ref.shape[1:]
+    tile_rows_count, tile_cols = eta_ref.shape
+    cells = (block_x, block_y, depth_cells)
+
+    def position(axis):
+        return lax.broadcasted_iota(jnp.int32, cells, axis)
+
+    links = (
+        (slab < slab_count - 1, slab + 1, pencil, slab > 0),
+        (slab > 0, slab - 1, pencil, slab < slab_count - 1),
+        (pencil < pencil_count - 1, slab, pencil + 1, pencil > 0),
+        (pencil > 0, slab, pencil - 1, pencil < pencil_count - 1),
+    )
+
+    def halo_copy(k, side, to_slab, to_pencil):
+        return pltpu.make_async_remote_copy(
+            src_ref=packed.at[k, side],
+            dst_ref=halo.at[k, side],
+            send_sem=halo_send.at[4 * k + side],
+            recv_sem=halo_recv.at[4 * k + side],
+            device_id={"slab": to_slab, "pencil": to_pencil},
+            device_id_type=pl.DeviceIdType.MESH,
+        )
+
+    def send_halo(k, velocity):
+        for c in range(3):
+            packed[k, 0, c] = velocity[c][block_x - 1]
+            packed[k, 1, c] = velocity[c][0]
+            packed[k, 2, c] = velocity[c][:, block_y - 1]
+            packed[k, 3, c] = velocity[c][:, 0]
+        for side, (sends, to_slab, to_pencil, _) in enumerate(links):
+
+            @pl.when(sends)
+            def _(side=side, to_slab=to_slab, to_pencil=to_pencil):
+                halo_copy(k, side, to_slab, to_pencil).start()
+
+    def wait_halo(k):
+        for side, (_, _, _, receives) in enumerate(links):
+
+            @pl.when(receives)
+            def _(side=side):
+                halo_copy(k, side, slab, pencil).wait_recv()
+
+    def end_halo(k):
+        for side, (sends, _, _, _) in enumerate(links):
+
+            @pl.when(sends)
+            def _(side=side):
+                halo_copy(k, side, slab, pencil).wait_send()
+
+    def predicted(k, velocity):
+        result = []
+        for c in range(3):
+            here = velocity[c]
+            minus_x = jnp.concatenate([halo[k, 0, c][None], here[:-1]], axis=0)
+            plus_x = jnp.concatenate([here[1:], halo[k, 1, c][None]], axis=0)
+            minus_y = jnp.where(
+                position(1) == 0, halo[k, 2, c][:, None], pltpu.roll(here, 1, 1)
+            )
+            plus_y = jnp.where(
+                position(1) == block_y - 1,
+                halo[k, 3, c][:, None],
+                pltpu.roll(here, block_y - 1, 1),
+            )
+            minus_z = jnp.where(position(2) == 0, 0.0, pltpu.roll(here, 1, 2))
+            plus_z = jnp.where(
+                position(2) == depth_cells - 1, 0.0, pltpu.roll(here, depth_cells - 1, 2)
+            )
+            laplace = (
+                plus_x + minus_x + (plus_y + minus_y) + (plus_z + minus_z) - 6.0 * here
+            )
+            advect = (
+                velocity[0] * (plus_x - minus_x)
+                + velocity[1] * (plus_y - minus_y)
+                + velocity[2] * (plus_z - minus_z)
+            )
+            result.append(here + TIME_STEP * (VISCOSITY * laplace - 0.5 * advect))
+        return result
+
+    def split_tile(ref):
+        @pl.loop(0, slab_count)
+        def _(i):
+            at = pl.multiple_of(i * rows, rows)
+            high, low = split(ref[pl.ds(at, rows)])
+            tile_split[pl.ds(at, rows)] = high
+            tile_split[pl.ds(pl.multiple_of(tile_rows_count + at, rows), rows)] = low
+
+    def pick(d):
+        both = jnp.dot(tile_split[...], pick_cols[d], preferred_element_type=jnp.float32)
+        row = lax.broadcasted_iota(jnp.int32, (tile_rows_count, capacity), 0)
+        found = both[:tile_rows_count] + both[tile_rows_count:]
+        return jnp.sum(jnp.where(row == row_index_ref[d], found, 0.0), axis=0, keepdims=True)
+
+    list_row = lax.broadcasted_iota(jnp.int32, (8, capacity), 0)
+
+    def prepare_flow():
+        split_tile(eta_ref)
+
+        @pl.loop(0, slab_count)
+        def _(d):
+            column = lax.broadcasted_iota(jnp.int32, (tile_cols, capacity), 0)
+            chosen = jnp.where(column == col_index_ref[d], 1.0, 0.0)
+            pick_cols[d] = chosen.astype(jnp.bfloat16)
+            slot = lax.broadcasted_iota(jnp.int32, (capacity, block_x * block_y), 0) + d * capacity
+            mixing = jnp.zeros(slot.shape, jnp.float32)
+            for q in range(stencil_ref.shape[0]):
+                mixing = mixing + jnp.where(slot == stencil_ref[q], share_ref[q], 0.0)
+            mix_high[d], mix_low[d] = split(mixing)
+
+        @pl.loop(0, slab_count)
+        def _(d):
+            picks[d] = jnp.where(list_row == 0, pick(d), 0.0)
+
+        wait_halo(0)
+        for c, value in enumerate(predicted(0, [velocity_ref[c] for c in range(3)])):
+            flow[c] = value
+
+    def finish_flow():
+        split_tile(out_ref)
+
+        @pl.loop(1, slab_count + 1)
+        def _(i):
+            d = lax.rem(slab + i, slab_count)
+            picks[d] = jnp.where(list_row == 1, pick(d), picks[d])
+
+            @pl.when(i < slab_count)
+            def _():
+                remote(picks.at[d], arrived.at[slab], fields + 3, d, pencil).start()
+
+        arrived[slab] = picks[slab]
+        all_of_slab(arrived, fields + 3).wait_recv()
+        surface = jnp.zeros((8, block_x * block_y), jnp.float32)
+        for r in range(slab_count):
+            high, low = split(arrived[r])
+            surface += jnp.dot(high, mix_high[r], preferred_element_type=jnp.float32) + (
+                jnp.dot(low, mix_high[r], preferred_element_type=jnp.float32)
+                + jnp.dot(high, mix_low[r], preferred_element_type=jnp.float32)
+            )
+        turned = surface.T
+        level = position(2).astype(jnp.float32)
+        decay = jnp.exp(-DEPTH_RATE * (depth_cells - 1.0 - level) / depth_cells)
+
+        def target(c):
+            spread = jnp.broadcast_to(turned[:, c : c + 1], (block_x * block_y, depth_cells))
+            return spread.reshape(cells) * decay
+
+        targets = [target(0), None, target(1)]
+        pos_x = (slab * block_x + position(0)).astype(jnp.float32)
+        pos_y = (pencil * block_y + position(1)).astype(jnp.float32)
+        reach_x = float(max(1, slab_count // 16) * block_x)
+        total_x, total_y = float(block_x * slab_count), float(block_y * pencil_count)
+        relax = jnp.maximum(
+            jnp.maximum(ramp_weight(pos_x, reach_x), ramp_weight(total_x - 1.0 - pos_x, reach_x)),
+            jnp.maximum(
+                ramp_weight(pos_y, float(block_y)),
+                ramp_weight(total_y - 1.0 - pos_y, float(block_y)),
+            ),
+        )
+
+        def blend(values):
+            blended = [(1.0 - relax) * value for value in values]
+            return [
+                value if aim is None else value + relax * aim
+                for value, aim in zip(blended, targets)
+            ]
+
+        velocity = blend([flow[c] for c in range(3)])
+        send_halo(1, velocity)
+        wait_halo(1)
+        for c, value in enumerate(blend(predicted(1, velocity))):
+            velocity_out[c] = value
+        end_halo(0)
+        end_halo(1)
+        all_of_slab(arrived, fields + 3).wait_send()
+
+    send_halo(0, [velocity_ref[c] for c in range(3)])
+
+    outer_x, outer_y = row_parts, col_parts
+    lane = own * columns + lax.broadcasted_iota(jnp.int32, (2 * INNER, columns), 1)
+
+    def wave(index, block, outer, length):
+        first = jnp.where(
+            index < INNER,
+            jnp.where(block == 0, 0, block),
+            jnp.where(block == 0, outer // 2, outer - block),
+        )
+        freq = first + outer * (index % INNER)
+        folded = jnp.minimum(freq, length - freq).astype(jnp.float32)
+        return 2.0 * math.pi / length * folded
+
+    wave_x = wave(lane % (2 * INNER), lane // (2 * INNER), outer_x, NXW)
+    place = lax.broadcasted_iota(jnp.int32, (2 * INNER, columns), 0)
+    for b in range(col_blocks):
+        wave_y = wave(place, jnp.full(place.shape, b, jnp.int32), outer_y, NYW)
+        magnitude[b] = jnp.sqrt(wave_x * wave_x + wave_y * wave_y)
 
     all_of_slab(potential, fields).wait_recv()
     over_rows(
@@ -399,9 +631,11 @@
     for copy in tables_in[2:]:
         copy.wait()
 
+    prepare_flow()
     forward_columns(0)
-    inverse_columns(1)
-    inverse_columns(2)
+    inverse_columns(1, True)
+    inverse_columns(2, False)
+    inverse_columns(3, False)
     all_of_slab(eta, fields + 1).wait_recv()
 
     def use_slope_one(at, parts):
@@ -436,19 +670,27 @@
         for p, value in enumerate(parts):
             part_of(total, p, at)[...] += value
 
-    inverse_columns(3)
+    middle = device_count // 2
+    all_of(1).wait_recv()
+    send(2, 1, device_count)
     inverse_rows(1, use_slope_one)
     finish_rows(4)
     inverse_rows(2, use_curve_one)
-    inverse_rows(3, use_cubic_one)
+    all_of(4).wait_recv()
+    send(3, 1, middle)
     forward_columns(4)
-    inverse_columns(5)
-    inverse_columns(6)
+    inverse_columns(5, True)
+    inverse_columns(6, False)
+    all_of(5).wait_recv()
+    send(6, 1, device_count)
     inverse_rows(5, use_slope_two)
     finish_rows(7)
     inverse_rows(6, use_curve_two)
+    all_of(7).wait_recv()
+    send(3, middle, device_count)
     forward_columns(7)
-    inverse_columns(8)
+    inverse_columns(8, True)
+    inverse_rows(3, use_cubic_one)
     inverse_rows(8, use_slope_three)
 
     send_slab(lambda to: total.at[to], back, fields + 2)
@@ -457,6 +699,7 @@
     for i in range(1, slab_count):
         source = lax.rem(slab + i, slab_count)
         out_ref[pl.ds(pl.multiple_of(source * rows, rows), rows)] = back[source]
+    finish_flow()
     for n in range(fields):
         all_of(n).wait_send()
     all_of_slab(potential, fields).wait_send()
@@ -470,7 +713,9 @@
     return jnp.asarray(high), jnp.asarray(low)
 
 
-def surface_chain(potential, eta, magnitude, slab_count, pencil_count):
+def whole_step(
+    potential, eta, velocity, points, counts, stencil, interp_weight, slab_count, pencil_count
+):
     tile_rows, tile_cols = eta.shape
     device_count = slab_count * pencil_count
     rows, columns = NYW // device_count, NXW // device_count
@@ -481,30 +726,64 @@
         *two_terms(col_table),
         *two_terms(np.ascontiguousarray(col_table.transpose(0, 2, 1))),
     ]
+    capacity = points.shape[1]
+    block_x, block_y, _ = velocity.shape[1:]
+    live = jnp.arange(capacity, dtype=jnp.int32)[None, :] < counts[:, None]
+    row_index = jnp.where(live, points // tile_cols, -1)[:, None, :]
+    col_index = (points % tile_cols)[:, None, :]
+    shares = interp_weight / jnp.sum(interp_weight, axis=0)
+    flat = (stencil.shape[0], 1, block_x * block_y)
+    spectrum = (col_table.shape[0], 2 * INNER, columns)
+    list_shape = (slab_count, 8, capacity)
+    halo_shape = (STEPS, 4, 3, block_x, velocity.shape[3])
     fields = 9
     strip = pltpu.VMEM((slab_count, rows, tile_cols), jnp.float32)
     vmem = pl.BlockSpec(memory_space=pltpu.VMEM)
     return pl.pallas_call(
         lambda *refs: surface_kernel(slab_count, pencil_count, *refs),
-        out_shape=jax.ShapeDtypeStruct((tile_rows, tile_cols), jnp.float32),
-        in_specs=[vmem] * 3 + [pl.BlockSpec(memory_space=pl.ANY)] * 6,
-        out_specs=vmem,
+        out_shape=(
+            jax.ShapeDtypeStruct((tile_rows, tile_cols), jnp.float32),
+            jax.ShapeDtypeStruct(velocity.shape, jnp.float32),
+        ),
+        in_specs=[vmem] * 7 + [pl.BlockSpec(memory_space=pl.ANY)] * 6,
+        out_specs=(vmem, vmem),
         scratch_shapes=[
             *(pltpu.VMEM(table.shape, jnp.bfloat16) for table in constants),
             *([strip] * 5),
             pltpu.VMEM(row_table.shape[:1] + (rows, 2 * INNER), jnp.float32),
-            pltpu.VMEM(magnitude.shape, jnp.float32),
-            pltpu.VMEM(magnitude.shape, jnp.float32),
+            pltpu.VMEM(spectrum, jnp.float32),
+            pltpu.VMEM(spectrum, jnp.float32),
+            pltpu.VMEM(spectrum, jnp.float32),
             pltpu.VMEM((fields, device_count, rows, columns), jnp.float32),
             pltpu.VMEM((fields, device_count, rows, columns), jnp.float32),
+            pltpu.VMEM((2 * tile_rows, tile_cols), jnp.bfloat16),
+            pltpu.VMEM((slab_count, tile_cols, capacity), jnp.bfloat16),
+            pltpu.VMEM((slab_count, capacity, block_x * block_y), jnp.bfloat16),
+            pltpu.VMEM((slab_count, capacity, block_x * block_y), jnp.bfloat16),
+            pltpu.VMEM(list_shape, jnp.float32),
+            pltpu.VMEM(list_shape, jnp.float32),
+            pltpu.VMEM(velocity.shape, jnp.float32),
+            pltpu.VMEM(halo_shape, jnp.float32),
+            pltpu.VMEM(halo_shape, jnp.float32),
             pltpu.SemaphoreType.DMA((6,)),
-            pltpu.SemaphoreType.DMA((fields + 3,)),
-            pltpu.SemaphoreType.DMA((fields + 3,)),
+            pltpu.SemaphoreType.DMA((fields + 4,)),
+            pltpu.SemaphoreType.DMA((fields + 4,)),
+            pltpu.SemaphoreType.DMA((4 * STEPS,)),
+            pltpu.SemaphoreType.DMA((4 * STEPS,)),
         ],
         compiler_params=pltpu.CompilerParams(
-            collective_id=0, has_side_effects=True, vmem_limit_bytes=56 * 1024 * 1024
+            collective_id=0, has_side_effects=True, vmem_limit_bytes=60 * 1024 * 1024
         ),
-    )(potential, eta, magnitude, *constants)
+    )(
+        potential,
+        eta,
+        velocity,
+        row_index,
+        col_index,
+        stencil.reshape(flat),
+        shares.reshape(flat),
+        *constants,
+    )
 
 
 def surface_plain(potential, eta, magnitude, row_table, column_table, slab_count):
@@ -600,6 +879,24 @@
     tile_rows, tile_cols = surface_eta.shape
     rows = NYW // device_count
     columns = NXW // device_count
+    if (
+        columns % 128 == 0
+        and rows % 16 == 0
+        and INNER % rows == 0
+        and velocity.shape[1] == velocity.shape[2]
+        and STEPS == 2
+    ):
+        return whole_step(
+            surface_potential,
+            surface_eta,
+            velocity,
+            send_point[0, 0],
+            send_count[0, 0],
+            stencil,
+            interp_weight,
+            slab_count,
+            pencil_count,
+        )
     own = pencil_index * slab_count + slab_index
     row_table, row_order = tables(NXW)
     column_table, column_order = tables(NYW)
@@ -607,14 +904,9 @@
     wave_x = lax.dynamic_slice(wave_x, (own * columns,), (columns,))
     wave_y = 2.0 * math.pi / NYW * jnp.asarray(column_order).astype(jnp.float32)[:, :, None]
     magnitude = jnp.sqrt(wave_x * wave_x + wave_y * wave_y)
-    if columns % 128 == 0 and rows % 16 == 0 and INNER % rows == 0:
-        vertical = surface_chain(
-            surface_potential, surface_eta, magnitude, slab_count, pencil_count
-        )
-    else:
-        vertical = surface_plain(
-            surface_potential, surface_eta, magnitude, row_table, column_table, slab_count
-        )
+    vertical = surface_plain(
+        surface_potential, surface_eta, magnitude, row_table, column_table, slab_count
+    )
 
     points = send_point[0, 0]
     capacity = points.shape[1]

time: 312 us -> 273 us (0.88)
  starting transfers between devices: 25.5 us -> 0 us
  matrix products: 11.6 us -> 0 us
    ppermute x8 -> x0, starting transfers between devices: 21.3 us -> none  [the longest x4 16 us: neighbours(): lax.ppermute(lax.slice_in_dim(shard, length - 1, length, axis=dim), axis,...]
    dot_general x3 -> x0, matrix products: 11.6 us -> none  [the longest x2 9.79 us: pick(): picked_rows = jnp.dot(row_pick, tile, precision=HIGH)]
    all_to_all x1 -> x0, starting transfers between devices: 4.23 us -> none  [on_device(): lax.all_to_all(picked, 'slab', split_axis=1, concat_axis=1, tiled=True)]
  transfers between devices with their start and end apart: 9 -> 0, of which waited for: 1 -> 0; matrix products, arithmetic and copies ran while one was open for 1% -> 0% of each run, Pallas kernels for 0% -> 0%
where the time goes in v3:
time: 273 us; the launch traced here: 272 us
  Pallas kernels  262 us (96%)
  local copies, waits for them, and re-layouts  5.18 us (2%)
  other arithmetic  4.22 us (2%)
    pallas_call x1, Pallas kernels, whole_step(): pl.pallas_call(lambda *refs: surface_kernel(slab_count, pencil_count, *re...  262 us

profile of v3, /device:TPU:0, one launch (start us, length us, event | category | flops | bytes accessed | tf_op | source)
XLA Modules:
  0.0 272.5 jit_solution(1259963835526410682)
XLA Ops:
  0.6 1.4 reshape.154.refs_5_
  2.1 0.8 reduce_sum.9
  2.8 1.3 and_select_fusion
  4.2 1.4 compare_select_fusion.refs_3_
  5.5 0.8 broadcast_divide_fusion
  6.3 0.7 reshape.155.refs_6_
  7.0 262.4 %shard_map.140 = (f32[512,512]{1,0:T(8,128)}, f32[3,16,16,128]{3,2,1,0:T(8,128)}) custom-call(f32[512,512]{1,0:T(8,128)} %refs_0_.1, f32[512,512]{1,0:T(8,128)} %refs_1_.1, f32[3,16,16,128]{3,2,1,0:T(8,128)} %refs_2_.1, s32[8,1,256]{2,1,0:T(1,128)} %compare_select_fusion.refs_3_, s32[8,1,256]{2,1,0:T(1,128)} %get-tuple-element.2.refs_4_, ...), custom_call_target="tpu_custom_call" | custom-call | tf_op jit(solution)/shard_map/pallas_call | solution.py:742
  269.4 0.0 copy-start
  269.4 2.3 copy.17
  271.7 0.0 copy-done
  271.7 0.7 copy.18
Async XLA Ops:
  269.4 2.3 copy-start

commit v4 on v3

--- a/solution.py
+++ b/solution.py
@@ -192,10 +192,9 @@
     potential_ref,
     eta_ref,
     velocity_ref,
-    row_index_ref,
-    col_index_ref,
-    stencil_ref,
-    share_ref,
+    points_ref,
+    counts_ref,
+    mixing_ref,
     row_high_in,
     row_low_in,
     col_high_in,
@@ -240,6 +239,7 @@
     pencil = lax.axis_index("pencil")
     device_count = slab_count * pencil_count
     own = pencil * slab_count + slab
+    own_col = slab * pencil_count + pencil
     rows = sent.shape[2]
     columns = sent.shape[3]
     per_block = 2 * INNER // columns
@@ -296,19 +296,26 @@
             device_id_type=pl.DeviceIdType.MESH,
         )
 
-    def start(n, to):
-        to_slab, to_pencil = lax.rem(to, slab_count), to // slab_count
-
+    def start_to_columns(n, to):
+        @pl.when(to != own_col)
+        def _():
+            remote(
+                sent.at[n, to], held.at[n, own], n, to // pencil_count, lax.rem(to, pencil_count)
+            ).start()
+
+    def start_to_rows(n, to):
         @pl.when(to != own)
         def _():
-            remote(sent.at[n, to], held.at[n, own], n, to_slab, to_pencil).start()
+            remote(
+                sent.at[n, to], held.at[n, own_col], n, lax.rem(to, slab_count), to // slab_count
+            ).start()
 
     def send(n, first, last):
         @pl.loop(first, last)
         def _(i):
             to_pencil, to_slab = partner(i)
             to = to_pencil * slab_count + to_slab
-            remote(sent.at[n, to], held.at[n, own], n, to_slab, to_pencil).start()
+            remote(sent.at[n, to], held.at[n, own_col], n, to_slab, to_pencil).start()
 
     def all_of(n):
         others = pl.ds(0, device_count - 1)
@@ -351,21 +358,21 @@
             piece_of(piece, at)[...] = value
 
     def finish_rows(n):
-        @pl.loop(0, row_blocks)
+        @pl.loop(0, row_blocks, unroll=2)
         def _(i):
-            b = lax.rem(i + own // per_block, row_blocks)
+            b = lax.rem(i + own_col // per_block, row_blocks)
             result = row_product(stage_rows[b], row_high, row_low, b, 0)
             for i in range(per_block):
                 sent[n, b * per_block + i] = result[:, i * columns : (i + 1) * columns]
-                start(n, b * per_block + i)
-
-        held[n, own] = sent[n, own]
+                start_to_columns(n, b * per_block + i)
+
+        held[n, own] = sent[n, own_col]
 
     def inverse_rows(n, use):
         if n in (2, 3, 6, 8):
             all_of(n).wait_recv()
 
-        @pl.loop(0, row_blocks)
+        @pl.loop(0, row_blocks, unroll=2)
         def _(b):
             values = jnp.concatenate(
                 [held[n, b * per_block + i] for i in range(per_block)], axis=1
@@ -394,12 +401,12 @@
 
         over_columns(body)
 
-        @pl.loop(0, col_blocks)
+        @pl.loop(0, col_blocks, unroll=2)
         def _(b):
             spectrum[b] = column_product(stage_cols[b], colt_high, colt_low, b)
 
     def inverse_columns(n, now):
-        @pl.loop(0, col_blocks)
+        @pl.loop(0, col_blocks, unroll=2)
         def _(b):
             values = spectrum[b] * magnitude[b]
             spectrum[b] = values
@@ -420,11 +427,11 @@
                     )
             if now:
                 for p in range(col_parts):
-                    start(n, p * per_part + q)
-
-        held[n, own] = sent[n, own]
-
-    capacity = row_index_ref.shape[2]
+                    start_to_rows(n, p * per_part + q)
+
+        held[n, own_col] = sent[n, own]
+
+    capacity = points_ref.shape[1]
     block_x, block_y, depth_cells = velocity_ref.shape[1:]
     tile_rows_count, tile_cols = eta_ref.shape
     cells = (block_x, block_y, depth_cells)
@@ -515,23 +522,31 @@
     def pick(d):
         both = jnp.dot(tile_split[...], pick_cols[d], preferred_element_type=jnp.float32)
         row = lax.broadcasted_iota(jnp.int32, (tile_rows_count, capacity), 0)
+        slot = lax.broadcasted_iota(jnp.int32, (1, capacity), 1)
+        live = slot < counts_ref[pl.ds(d, 1)]
+        wanted = jnp.where(live, points_ref[pl.ds(d, 1)] // tile_cols, -1)
         found = both[:tile_rows_count] + both[tile_rows_count:]
-        return jnp.sum(jnp.where(row == row_index_ref[d], found, 0.0), axis=0, keepdims=True)
+        return jnp.sum(jnp.where(row == wanted, found, 0.0), axis=0, keepdims=True)
 
     list_row = lax.broadcasted_iota(jnp.int32, (8, capacity), 0)
 
     def prepare_flow():
         split_tile(eta_ref)
+        mixing_in = mixing_ref[...]
+        points_each = mixing_in.shape[0] // 2
+        weights = [mixing_in[points_each + q][None] for q in range(points_each)]
+        shares = [weight / sum(weights[1:], weights[0]) for weight in weights]
+        slots = [mixing_in[q][None].astype(jnp.int32) for q in range(points_each)]
 
         @pl.loop(0, slab_count)
         def _(d):
             column = lax.broadcasted_iota(jnp.int32, (tile_cols, capacity), 0)
-            chosen = jnp.where(column == col_index_ref[d], 1.0, 0.0)
+            chosen = jnp.where(column == points_ref[pl.ds(d, 1)] % tile_cols, 1.0, 0.0)
             pick_cols[d] = chosen.astype(jnp.bfloat16)
             slot = lax.broadcasted_iota(jnp.int32, (capacity, block_x * block_y), 0) + d * capacity
             mixing = jnp.zeros(slot.shape, jnp.float32)
-            for q in range(stencil_ref.shape[0]):
-                mixing = mixing + jnp.where(slot == stencil_ref[q], share_ref[q], 0.0)
+            for q in range(points_each):
+                mixing = mixing + jnp.where(slot == slots[q], shares[q], 0.0)
             mix_high[d], mix_low[d] = split(mixing)
 
         @pl.loop(0, slab_count)
@@ -603,7 +618,7 @@
     send_halo(0, [velocity_ref[c] for c in range(3)])
 
     outer_x, outer_y = row_parts, col_parts
-    lane = own * columns + lax.broadcasted_iota(jnp.int32, (2 * INNER, columns), 1)
+    lane = own_col * columns + lax.broadcasted_iota(jnp.int32, (2 * INNER, columns), 1)
 
     def wave(index, block, outer, length):
         first = jnp.where(
@@ -728,11 +743,8 @@
     ]
     capacity = points.shape[1]
     block_x, block_y, _ = velocity.shape[1:]
-    live = jnp.arange(capacity, dtype=jnp.int32)[None, :] < counts[:, None]
-    row_index = jnp.where(live, points // tile_cols, -1)[:, None, :]
-    col_index = (points % tile_cols)[:, None, :]
-    shares = interp_weight / jnp.sum(interp_weight, axis=0)
-    flat = (stencil.shape[0], 1, block_x * block_y)
+    mixing = jnp.concatenate([stencil.astype(jnp.float32), interp_weight])
+    mixing = mixing.reshape(-1, block_x * block_y)
     spectrum = (col_table.shape[0], 2 * INNER, columns)
     list_shape = (slab_count, 8, capacity)
     halo_shape = (STEPS, 4, 3, block_x, velocity.shape[3])
@@ -745,7 +757,7 @@
             jax.ShapeDtypeStruct((tile_rows, tile_cols), jnp.float32),
             jax.ShapeDtypeStruct(velocity.shape, jnp.float32),
         ),
-        in_specs=[vmem] * 7 + [pl.BlockSpec(memory_space=pl.ANY)] * 6,
+        in_specs=[vmem] * 6 + [pl.BlockSpec(memory_space=pl.ANY)] * 6,
         out_specs=(vmem, vmem),
         scratch_shapes=[
             *(pltpu.VMEM(table.shape, jnp.bfloat16) for table in constants),
@@ -778,10 +790,9 @@
         potential,
         eta,
         velocity,
-        row_index,
-        col_index,
-        stencil.reshape(flat),
-        shares.reshape(flat),
+        points,
+        counts[:, None],
+        mixing,
         *constants,
     )
 

time: 273 us -> 271 us (level)
  no operation moved by 1% of the time
where the time goes in v4:
time: 271 us
  Pallas kernels  264 us (97%)
  local copies, waits for them, and re-layouts  5.07 us (2%)
    pallas_call x1, Pallas kernels, whole_step(): pl.pallas_call(lambda *refs: surface_kernel(slab_count, pencil_count, *re...  264 us

profile of v4, /device:TPU:0, one launch (start us, length us, event | category | flops | bytes accessed | tf_op | source)
XLA Modules:
  0.0 270.8 jit_solution(15248624052862914251)
XLA Ops:
  0.6 1.3 copy.15.refs_4_
  2.0 0.8 convert_element_type.3
  2.7 0.8 pad_maximum_fusion
  3.5 0.7 reshape.7.refs_5_
  4.2 263.6 %shard_map.140 = (f32[512,512]{1,0:T(8,128)}, f32[3,16,16,128]{3,2,1,0:T(8,128)}) custom-call(f32[512,512]{1,0:T(8,128)} %refs_0_.1, f32[512,512]{1,0:T(8,128)} %refs_1_.1, f32[3,16,16,128]{3,2,1,0:T(8,128)} %refs_2_.1, s32[8,256]{1,0:T(8,128)} %bitcast.2, s32[8,1]{1,0:T(8,128)} %copy.15.refs_4_, f32[8,256]{1,0:T(8,128)} %reshape.7.refs_5_, ...), custom_call_target="tpu_custom_call" | custom-call | tf_op jit(solution)/shard_map/pallas_call | solution.py:754
  267.7 0.0 copy-start
  267.7 2.3 copy.18
  270.1 0.0 copy-done
  270.1 0.7 copy.19
Async XLA Ops:
  267.7 2.3 copy-start

commit v5 on v4

--- a/solution.py
+++ b/solution.py
@@ -331,13 +331,43 @@
         return remote(others, others, n, slab, pencil)
 
     fields = sent.shape[0]
-
-    def tile_rows(ref):
-        return lambda to: ref.at[pl.ds(pl.multiple_of(to * rows, rows), rows)]
+    half_rows = rows // 2
+    halves = (pl.ds(0, half_rows), pl.ds(half_rows, half_rows))
+    potential_sems = (fields, fields + 4)
+    first_sems = (0, fields + 5)
+    last_sems = (8, fields + 6)
+    back_sems = (fields + 2, fields + 7)
+
+    def tile_rows(ref, half=None):
+        if half is None:
+            return lambda to: ref.at[pl.ds(pl.multiple_of(to * rows, rows), rows)]
+        return lambda to: ref.at[
+            pl.ds(pl.multiple_of(to * rows + half * half_rows, half_rows), half_rows)
+        ]
+
+    def send_slab_half(source_of, target, half, sems):
+        for i in range(1, slab_count):
+            to = lax.rem(slab + i, slab_count)
+            remote(
+                source_of(to), target.at[slab, halves[half]], sems[half], to, pencil
+            ).start()
+
+    def all_of_slab_half(target, half, sems):
+        others = target.at[pl.ds(0, slab_count - 1), halves[half]]
+        return remote(others, others, sems[half], slab, pencil)
+
+    def all_of_half(n, half, sems):
+        others = pl.ds(0, device_count - 1)
+        return remote(
+            sent.at[n, others, halves[half]],
+            held.at[n, others, halves[half]],
+            sems[half],
+            slab,
+            pencil,
+        )
 
     own_rows = pl.ds(pl.multiple_of(slab * rows, rows), rows)
-    send_slab(tile_rows(potential_ref), potential, fields)
-    send_slab(tile_rows(eta_ref), eta, fields + 1)
+    send_slab_half(tile_rows(potential_ref, 0), potential, 0, potential_sems)
     potential[slab] = potential_ref[own_rows]
     eta[slab] = eta_ref[own_rows]
 
@@ -348,8 +378,11 @@
     def piece_of(piece, at):
         return stage_rows.at[piece // 2, at, pl.ds(piece % 2 * INNER, INNER)]
 
-    def over_rows(body):
-        @pl.loop(0, rows // step)
+    def over_rows(body, half=None):
+        start = 0 if half is None else half * half_rows
+        stop = rows if half is None else start + half_rows
+
+        @pl.loop(start // step, stop // step)
         def _(i):
             body(pl.ds(pl.multiple_of(i * step, step), step))
 
@@ -358,7 +391,7 @@
             piece_of(piece, at)[...] = value
 
     def finish_rows(n):
-        @pl.loop(0, row_blocks, unroll=2)
+        @pl.loop(0, row_blocks)
         def _(i):
             b = lax.rem(i + own_col // per_block, row_blocks)
             result = row_product(stage_rows[b], row_high, row_low, b, 0)
@@ -368,11 +401,61 @@
 
         held[n, own] = sent[n, own_col]
 
+    def finish_rows_half(n, half, sems):
+        part = halves[half]
+
+        @pl.loop(0, row_blocks)
+        def _(i):
+            b = lax.rem(i + own_col // per_block, row_blocks)
+            result = row_product(stage_rows[b, part], row_high, row_low, b, 0)
+            for j in range(per_block):
+                to = b * per_block + j
+                sent[n, to, part] = result[:, j * columns : (j + 1) * columns]
+
+                @pl.when(to != own_col)
+                def _(to=to):
+                    remote(
+                        sent.at[n, to, part],
+                        held.at[n, own, part],
+                        sems[half],
+                        to // pencil_count,
+                        lax.rem(to, pencil_count),
+                    ).start()
+
+        held[n, own, part] = sent[n, own_col, part]
+
+    def inverse_rows_half(n, use, half, sems):
+        part = halves[half]
+        all_of_half(n, half, sems).wait_recv()
+
+        @pl.loop(0, row_blocks)
+        def _(b):
+            values = jnp.concatenate(
+                [held[n, b * per_block + i, part] for i in range(per_block)], axis=1
+            )
+            stage_rows[b, part] = row_product(values, row_high, row_low, b, 1)
+
+        def body(at):
+            use(at, outer_dft_transposed([piece_of(p, at)[...] for p in range(row_parts)]))
+
+        over_rows(body, half)
+
+    def send_half_to_rows(n, half, sems):
+        part = halves[half]
+
+        @pl.loop(1, device_count)
+        def _(i):
+            to_pencil, to_slab = partner(i)
+            to = to_pencil * slab_count + to_slab
+            remote(
+                sent.at[n, to, part], held.at[n, own_col, part], sems[half], to_slab, to_pencil
+            ).start()
+
     def inverse_rows(n, use):
         if n in (2, 3, 6, 8):
             all_of(n).wait_recv()
 
-        @pl.loop(0, row_blocks, unroll=2)
+        @pl.loop(0, row_blocks)
         def _(b):
             values = jnp.concatenate(
                 [held[n, b * per_block + i] for i in range(per_block)], axis=1
@@ -390,9 +473,6 @@
             body(i // 2, pl.multiple_of(lax.rem(i, 2) * (rows // 2), rows // 2))
 
     def forward_columns(n):
-        if n == 0:
-            all_of(n).wait_recv()
-
         def body(q, start):
             parts = [held[n, p * per_part + q, pl.ds(start, rows // 2)] for p in range(col_parts)]
             for piece, value in enumerate(outer_dft(parts)):
@@ -401,12 +481,12 @@
 
         over_columns(body)
 
-        @pl.loop(0, col_blocks, unroll=2)
+        @pl.loop(0, col_blocks)
         def _(b):
             spectrum[b] = column_product(stage_cols[b], colt_high, colt_low, b)
 
     def inverse_columns(n, now):
-        @pl.loop(0, col_blocks, unroll=2)
+        @pl.loop(0, col_blocks)
         def _(b):
             values = spectrum[b] * magnitude[b]
             spectrum[b] = values
@@ -415,7 +495,7 @@
         @pl.loop(0, per_part)
         def _(i):
             q = lax.rem(i + own, per_part)
-            for half in range(2):
+            for half in (0, 1):
                 offset = half * (rows // 2)
                 pieces = []
                 for piece in range(col_parts):
@@ -636,17 +716,28 @@
         wave_y = wave(place, jnp.full(place.shape, b, jnp.int32), outer_y, NYW)
         magnitude[b] = jnp.sqrt(wave_x * wave_x + wave_y * wave_y)
 
-    all_of_slab(potential, fields).wait_recv()
-    over_rows(
-        lambda at: begin_rows([part_of(potential, p, at)[...] for p in range(row_parts)], at)
-    )
+    def begin_potential(half):
+        over_rows(
+            lambda at: begin_rows([part_of(potential, p, at)[...] for p in range(row_parts)], at),
+            half,
+        )
+
+    all_of_slab_half(potential, 0, potential_sems).wait_recv()
+    send_slab_half(tile_rows(potential_ref, 1), potential, 1, potential_sems)
+    begin_potential(0)
     tables_in[0].wait()
     tables_in[1].wait()
-    finish_rows(0)
+    finish_rows_half(0, 0, first_sems)
+    all_of_slab_half(potential, 1, potential_sems).wait_recv()
+    begin_potential(1)
+    finish_rows_half(0, 1, first_sems)
     for copy in tables_in[2:]:
         copy.wait()
 
     prepare_flow()
+    all_of_half(0, 0, first_sems).wait_recv()
+    all_of_half(0, 1, first_sems).wait_recv()
+    send_slab(tile_rows(eta_ref), eta, fields + 1)
     forward_columns(0)
     inverse_columns(1, True)
     inverse_columns(2, False)
@@ -704,22 +795,30 @@
     all_of(7).wait_recv()
     send(3, middle, device_count)
     forward_columns(7)
-    inverse_columns(8, True)
+    inverse_columns(8, False)
+    send_half_to_rows(8, 0, last_sems)
+    all_of_half(8, 0, last_sems).wait_send()
+    send_half_to_rows(8, 1, last_sems)
     inverse_rows(3, use_cubic_one)
-    inverse_rows(8, use_slope_three)
-
-    send_slab(lambda to: total.at[to], back, fields + 2)
+    for half in (0, 1):
+        inverse_rows_half(8, use_slope_three, half, last_sems)
+        send_slab_half(lambda to, half=half: total.at[to, halves[half]], back, half, back_sems)
     out_ref[own_rows] = total[slab]
-    all_of_slab(back, fields + 2).wait_recv()
-    for i in range(1, slab_count):
-        source = lax.rem(slab + i, slab_count)
-        out_ref[pl.ds(pl.multiple_of(source * rows, rows), rows)] = back[source]
+    for half in (0, 1):
+        all_of_slab_half(back, half, back_sems).wait_recv()
+        for i in range(1, slab_count):
+            source = lax.rem(slab + i, slab_count)
+            at = pl.multiple_of(source * rows + half * half_rows, half_rows)
+            out_ref[pl.ds(at, half_rows)] = back[source, halves[half]]
     finish_flow()
-    for n in range(fields):
+    for n in range(1, fields - 1):
         all_of(n).wait_send()
-    all_of_slab(potential, fields).wait_send()
     all_of_slab(eta, fields + 1).wait_send()
-    all_of_slab(back, fields + 2).wait_send()
+    all_of_half(8, 1, last_sems).wait_send()
+    for half in (0, 1):
+        all_of_half(0, half, first_sems).wait_send()
+        all_of_slab_half(potential, half, potential_sems).wait_send()
+        all_of_slab_half(back, half, back_sems).wait_send()
 
 
 def two_terms(table):
@@ -778,8 +877,8 @@
             pltpu.VMEM(halo_shape, jnp.float32),
             pltpu.VMEM(halo_shape, jnp.float32),
             pltpu.SemaphoreType.DMA((6,)),
-            pltpu.SemaphoreType.DMA((fields + 4,)),
-            pltpu.SemaphoreType.DMA((fields + 4,)),
+            pltpu.SemaphoreType.DMA((fields + 8,)),
+            pltpu.SemaphoreType.DMA((fields + 8,)),
             pltpu.SemaphoreType.DMA((4 * STEPS,)),
             pltpu.SemaphoreType.DMA((4 * STEPS,)),
         ],

time: 271 us -> 265 us (0.978)
  Pallas kernels: 264 us -> 257 us
    pallas_call x1, Pallas kernels: 264 us -> 257 us  [whole_step(): pl.pallas_call(lambda *refs: surface_kernel(slab_count, pencil_count, *re...]
where the time goes in v5:
time: 265 us
  Pallas kernels  257 us (97%)
  local copies, waits for them, and re-layouts  5.07 us (2%)
    pallas_call x1, Pallas kernels, whole_step(): pl.pallas_call(lambda *refs: surface_kernel(slab_count, pencil_count, *re...  257 us

profile of v5, /device:TPU:0, one launch (start us, length us, event | category | flops | bytes accessed | tf_op | source)
XLA Modules:
  0.0 264.7 jit_solution(3114581197455627918)
XLA Ops:
  0.6 1.3 copy.15.refs_4_
  2.0 0.8 convert_element_type.3
  2.7 0.8 pad_maximum_fusion
  3.5 0.7 reshape.7.refs_5_
  4.2 257.5 %shard_map.140 = (f32[512,512]{1,0:T(8,128)}, f32[3,16,16,128]{3,2,1,0:T(8,128)}) custom-call(f32[512,512]{1,0:T(8,128)} %refs_0_.1, f32[512,512]{1,0:T(8,128)} %refs_1_.1, f32[3,16,16,128]{3,2,1,0:T(8,128)} %refs_2_.1, s32[8,256]{1,0:T(8,128)} %bitcast.2, s32[8,1]{1,0:T(8,128)} %copy.15.refs_4_, f32[8,256]{1,0:T(8,128)} %reshape.7.refs_5_, ...), custom_call_target="tpu_custom_call" | custom-call | tf_op jit(solution)/shard_map/pallas_call | solution.py:853
  261.6 0.0 copy-start
  261.6 2.3 copy.18
  264.0 0.0 copy-done
  264.0 0.7 copy.19
Async XLA Ops:
  261.6 2.3 copy-start

commit v6 on v5

--- a/solution.py
+++ b/solution.py
@@ -506,8 +506,9 @@
                         1.0 / (NXW * NYW)
                     )
             if now:
+                turn = (pencil + 1) * (col_parts // pencil_count)
                 for p in range(col_parts):
-                    start_to_rows(n, p * per_part + q)
+                    start_to_rows(n, lax.rem(p + turn, col_parts) * per_part + q)
 
         held[n, own_col] = sent[n, own]
 
@@ -603,7 +604,9 @@
         both = jnp.dot(tile_split[...], pick_cols[d], preferred_element_type=jnp.float32)
         row = lax.broadcasted_iota(jnp.int32, (tile_rows_count, capacity), 0)
         slot = lax.broadcasted_iota(jnp.int32, (1, capacity), 1)
-        live = slot < counts_ref[pl.ds(d, 1)]
+        counts = counts_ref[...]
+        toward = lax.broadcasted_iota(jnp.int32, counts.shape, 1) == d
+        live = slot < jnp.sum(jnp.where(toward, counts, 0), axis=1, keepdims=True)
         wanted = jnp.where(live, points_ref[pl.ds(d, 1)] // tile_cols, -1)
         found = both[:tile_rows_count] + both[tile_rows_count:]
         return jnp.sum(jnp.where(row == wanted, found, 0.0), axis=0, keepdims=True)
@@ -777,8 +780,9 @@
             part_of(total, p, at)[...] += value
 
     middle = device_count // 2
+    all_of(1).wait_send()
+    send(2, 1, device_count)
     all_of(1).wait_recv()
-    send(2, 1, device_count)
     inverse_rows(1, use_slope_one)
     finish_rows(4)
     inverse_rows(2, use_curve_one)
@@ -787,8 +791,9 @@
     forward_columns(4)
     inverse_columns(5, True)
     inverse_columns(6, False)
+    all_of(5).wait_send()
+    send(6, 1, device_count)
     all_of(5).wait_recv()
-    send(6, 1, device_count)
     inverse_rows(5, use_slope_two)
     finish_rows(7)
     inverse_rows(6, use_curve_two)
@@ -811,7 +816,7 @@
             at = pl.multiple_of(source * rows + half * half_rows, half_rows)
             out_ref[pl.ds(at, half_rows)] = back[source, halves[half]]
     finish_flow()
-    for n in range(1, fields - 1):
+    for n in (2, 3, 4, 6, 7):
         all_of(n).wait_send()
     all_of_slab(eta, fields + 1).wait_send()
     all_of_half(8, 1, last_sems).wait_send()
@@ -890,7 +895,7 @@
         eta,
         velocity,
         points,
-        counts[:, None],
+        counts[None],
         mixing,
         *constants,
     )

time: 265 us -> 261 us (0.985)
    pallas_call x1, Pallas kernels: 257 us -> 255 us  [whole_step(): pl.pallas_call(lambda *refs: surface_kernel(slab_count, pencil_count, *re...]
where the time goes in v6:
time: 261 us
  Pallas kernels  255 us (98%)
  local copies, waits for them, and re-layouts  3.75 us (1%)
    pallas_call x1, Pallas kernels, whole_step(): pl.pallas_call(lambda *refs: surface_kernel(slab_count, pencil_count, *re...  255 us

profile of v6, /device:TPU:0, one launch (start us, length us, event | category | flops | bytes accessed | tf_op | source)
XLA Modules:
  0.0 260.6 jit_solution(17795191568193601415)
XLA Ops:
  0.6 0.8 convert_element_type.3
  1.4 0.8 pad_maximum_fusion
  2.2 0.7 reshape.7.refs_5_
  2.8 254.7 %shard_map.140 = (f32[512,512]{1,0:T(8,128)}, f32[3,16,16,128]{3,2,1,0:T(8,128)}) custom-call(f32[512,512]{1,0:T(8,128)} %refs_0_.1, f32[512,512]{1,0:T(8,128)} %refs_1_.1, f32[3,16,16,128]{3,2,1,0:T(8,128)} %refs_2_.1, s32[8,256]{1,0:T(8,128)} %bitcast.2, s32[1,8]{1,0:T(1,128)} %bitcast.3, f32[8,256]{1,0:T(8,128)} %reshape.7.refs_5_, ...), custom_call_target="tpu_custom_call" | custom-call | tf_op jit(solution)/shard_map/pallas_call | solution.py:858
  257.6 0.0 copy-start
  257.6 2.3 copy.17
  259.9 0.0 copy-done
  259.9 0.7 copy.18
Async XLA Ops:
  257.6 2.3 copy-start
